TPU v7x, 32 devices: a whole 2x2x4 slice. The times are simulated.
32 devices in a mesh: groups: 2 (over y), freq: 4 (over z), read: 2 (over x), pair: 2 (over core).
Axes of the slice: x: 2, y: 2, z: 4, core: 2. Of those that a mesh axis runs over, the one named last changes fastest.
Arguments:
- exposures: float32 [8, 2048, 2048], P(('groups', 'read', 'pair'), 'freq'), parts along dimension 0, may hold values from -6 to 6
- stamps: float32 [8, 16, 16], P('groups'), parts along dimension 0, may hold values from -1 to 1, as said below
- zero_point: float32 [8], P('groups'), parts along dimension 0, may hold values from 0.5 to 2
- noise_var: float32 [8], P('groups'), parts along dimension 0, may hold values from 0.25 to 4
- footprint: int32 [8, 2], P('groups'), parts along dimension 0, may hold values from 0 to 2048, as said below
- accept: int32 [8], P('groups'), parts along dimension 0, may hold values from 0 to 1, as said below
- assign: int32 [8], P('groups'), parts along dimension 0, may hold values from 0 to 3, each once
Outputs:
- coadd: float32 [2, 4096, 1024], P(None, ('groups', 'read', 'pair'), 'freq'), parts along dimension 1
There are 2 independent parts, one for each index of `groups`. A program takes and returns all parts, laid end to end along the dimension named above; each array names one. Nothing has to cross between parts.
Inputs may be any that keep to these rules, and one draw needn't show every extreme that they name: `stamps`: each stamp is 1 at row 8 and column 8, and the absolute values of its other entries sum to at most 0.9. For every exposure footprint[e, 0] < footprint[e, 1] and the two differ by at least 512; some exposure covers all 2048 rows. `accept`: at least one exposure is rejected, and at least one exposure that covers all 2048 rows is accepted. `assign`: each exposure sits in exactly one slot.
All inputs are finite; a program needn't handle non-finite values.
Results may differ from a plain program's by a relative error of at most 0.0001.
Values sent between devices are 32-bit elements; how exact they have to be, the bound alone decides.
A program may use at most 64 MiB of HBM per device.

v0:
```python
import math

import jax
import jax.numpy as jnp
from jax import lax
from jax.sharding import PartitionSpec as P

HIGHEST = lax.Precision.HIGHEST
TWO_PI = 2.0 * math.pi
LANES = 128


def with_halo(block, sides, width):
    for axis, dim in sides:
        count = lax.axis_size(axis)
        forward = [(i, i + 1) for i in range(count - 1)]
        backward = [(target, source) for source, target in forward]
        low = lax.ppermute(
            lax.slice_in_dim(block, block.shape[dim] - width, None, axis=dim), axis, forward
        )
        high = lax.ppermute(lax.slice_in_dim(block, 0, width, axis=dim), axis, backward)
        block = jnp.concatenate([low, block, high], axis=dim)
    return block


def phase_table(left_ids, right_ids, modulus):
    product = left_ids[:, None] * right_ids[None, :] % modulus
    return product.astype(jnp.float32) * (TWO_PI / modulus)


def fourier(real_in, imag_in, length):
    outer = length // LANES
    lead = real_in.shape[:-1]
    outer_ids = jnp.arange(outer, dtype=jnp.int32)
    lane_ids = jnp.arange(LANES, dtype=jnp.int32)
    short_phase = phase_table(outer_ids, outer_ids, outer)
    cos_a = jnp.cos(short_phase)
    sin_a = jnp.sin(short_phase)
    shaped_re = real_in.reshape(lead + (outer, LANES))
    first_re = jnp.einsum("...ab,ad->...db", shaped_re, cos_a, precision=HIGHEST)
    first_im = -jnp.einsum("...ab,ad->...db", shaped_re, sin_a, precision=HIGHEST)
    if imag_in is not None:
        shaped_im = imag_in.reshape(lead + (outer, LANES))
        first_re = first_re + jnp.einsum("...ab,ad->...db", shaped_im, sin_a, precision=HIGHEST)
        first_im = first_im + jnp.einsum("...ab,ad->...db", shaped_im, cos_a, precision=HIGHEST)
    twist = phase_table(outer_ids, lane_ids, length)
    twist_cos = jnp.cos(twist)
    twist_sin = jnp.sin(twist)
    mid_re = first_re * twist_cos + first_im * twist_sin
    mid_im = first_im * twist_cos - first_re * twist_sin
    lane_phase = phase_table(lane_ids, lane_ids, LANES)
    cos_b = jnp.cos(lane_phase)
    sin_b = jnp.sin(lane_phase)
    out_re = jnp.einsum("...db,bc->...cd", mid_re, cos_b, precision=HIGHEST) + jnp.einsum(
        "...db,bc->...cd", mid_im, sin_b, precision=HIGHEST
    )
    out_im = jnp.einsum("...db,bc->...cd", mid_im, cos_b, precision=HIGHEST) - jnp.einsum(
        "...db,bc->...cd", mid_re, sin_b, precision=HIGHEST
    )
    return (out_re.reshape(lead + (length,)), out_im.reshape(lead + (length,)))


def pack_blocks(real_part, imag_part, blocks):
    lead = real_part.shape[:-1]
    slice_width = real_part.shape[-1] // blocks
    both = jnp.stack(
        [
            real_part.reshape(lead + (blocks, slice_width)),
            imag_part.reshape(lead + (blocks, slice_width)),
        ],
        axis=-2,
    )
    return both.reshape(lead + (blocks * 2 * slice_width,))


def stamp_columns(stamp_set, freq_ids, image_width):
    stamp_len = stamp_set.shape[1]
    offsets = jnp.arange(stamp_len, dtype=jnp.int32) - stamp_len // 2
    phases = phase_table(jnp.mod(offsets, image_width), freq_ids, image_width)
    q_real = jnp.einsum("nab,bp->nap", stamp_set, jnp.cos(phases), precision=HIGHEST)
    q_imag = -jnp.einsum("nab,bp->nap", stamp_set, jnp.sin(phases), precision=HIGHEST)
    return (q_real, q_imag)


def psf_spectrum(stamp_set, rows_u, freq_ids, image_height, image_width):
    stamp_len = stamp_set.shape[1]
    q_real, q_imag = stamp_columns(stamp_set, freq_ids, image_width)
    offsets = jnp.arange(stamp_len, dtype=jnp.int32) - stamp_len // 2
    phases = phase_table(rows_u, jnp.mod(offsets, image_height), image_height)
    cos_u = jnp.cos(phases)
    sin_u = jnp.sin(phases)
    p_real = jnp.einsum("ma,nap->nmp", cos_u, q_real, precision=HIGHEST) + jnp.einsum(
        "ma,nap->nmp", sin_u, q_imag, precision=HIGHEST
    )
    p_imag = jnp.einsum("ma,nap->nmp", cos_u, q_imag, precision=HIGHEST) - jnp.einsum(
        "ma,nap->nmp", sin_u, q_real, precision=HIGHEST
    )
    return (p_real, p_imag)


def per_device(exposures, stamps, zero_point, noise_var, footprint, accept, assign):
    exp_dev, rows_dev, image_width = exposures.shape
    freq_count = lax.axis_size("freq")
    reader_count = lax.axis_size(("read", "pair"))
    image_height = rows_dev * freq_count
    half_width = image_width // 2
    per_freq = half_width // freq_count
    out_rows = image_height // reader_count
    count_all = assign.shape[0]
    freq_at = lax.axis_index("freq")
    reader_at = lax.axis_index(("read", "pair"))
    labels = jnp.arange(count_all, dtype=jnp.int32)
    slot_ids = reader_at * exp_dev + jnp.arange(exp_dev, dtype=jnp.int32)
    owner_id = jnp.sum(jnp.where(slot_ids[:, None] == labels[None, :], assign[None, :], 0), axis=1)
    chosen = owner_id[:, None] == labels[None, :]
    low_row = jnp.sum(jnp.where(chosen, footprint[None, :, 0], 0), axis=1)
    high_row = jnp.sum(jnp.where(chosen, footprint[None, :, 1], 0), axis=1)
    accepted = accept.astype(jnp.float32)
    numer_weight = accepted * zero_point / noise_var
    denom_weight = accepted * zero_point * zero_point / noise_var
    local_weight = jnp.sum(jnp.where(chosen, numer_weight[None, :], 0.0), axis=1)
    local_stamps = jnp.sum(jnp.where(chosen[:, :, None, None], stamps[None], 0.0), axis=1)
    padded = with_halo(exposures, (("freq", 1),), 1)
    zero_col = jnp.zeros((exp_dev, rows_dev, 1), jnp.float32)
    left_cells = jnp.concatenate([zero_col, exposures[:, :, :-1]], axis=2)
    right_cells = jnp.concatenate([exposures[:, :, 1:], zero_col], axis=2)
    row_global = freq_at * rows_dev + jnp.arange(rows_dev, dtype=jnp.int32)
    inside = (row_global[None, :] >= low_row[:, None]) & (row_global[None, :] < high_row[:, None])
    beside = padded[:, :-2] + padded[:, 2:] + left_cells + right_cells
    cleaned = jnp.where(inside[:, :, None], exposures - 0.25 * beside, 0.0)
    rows_out = reader_at * out_rows + jnp.arange(out_rows, dtype=jnp.int32)
    cols_own = freq_at * per_freq + jnp.arange(per_freq, dtype=jnp.int32)
    all_real, all_imag = psf_spectrum(stamps, rows_out, cols_own, image_height, image_width)
    denom = jnp.einsum(
        "n,nmp->mp", denom_weight, all_real * all_real + all_imag * all_imag, precision=HIGHEST
    )
    spec_re, spec_im = fourier(cleaned, None, image_width)
    packed = pack_blocks(spec_re[:, :, :half_width], spec_im[:, :, :half_width], freq_count)
    spectra = jnp.transpose(packed, (1, 0, 2)).reshape(rows_dev, exp_dev, freq_count, 2 * per_freq)
    regrouped = lax.all_to_all(spectra, "freq", split_axis=2, concat_axis=0, tiled=True)
    regrouped = regrouped.reshape(image_height, exp_dev, 2, per_freq)
    col_re = jnp.transpose(regrouped[:, :, 0], (1, 2, 0))
    col_im = jnp.transpose(regrouped[:, :, 1], (1, 2, 0))
    grid_re, grid_im = fourier(col_re, col_im, image_height)
    rows_u = jnp.arange(out_rows * lax.axis_size(("read", "pair")), dtype=jnp.int32)
    kernel_real, kernel_imag = psf_spectrum(
        local_stamps, rows_u, cols_own, image_height, image_width
    )
    term_real = jnp.einsum(
        "e,emp,epm->mp", local_weight, kernel_real, grid_re, precision=HIGHEST
    ) + jnp.einsum("e,emp,epm->mp", local_weight, kernel_imag, grid_im, precision=HIGHEST)
    term_imag = jnp.einsum(
        "e,emp,epm->mp", local_weight, kernel_real, grid_im, precision=HIGHEST
    ) - jnp.einsum("e,emp,epm->mp", local_weight, kernel_imag, grid_re, precision=HIGHEST)
    summed = lax.psum_scatter(
        jnp.concatenate([term_real, term_imag], axis=1),
        ("read", "pair"),
        scatter_dimension=0,
        tiled=True,
    )
    numer_real = summed[:, :per_freq]
    numer_imag = summed[:, per_freq:]
    scale = 1.0 / math.sqrt(image_height * image_width)
    root = jnp.sqrt(denom)
    return jnp.stack([numer_real / root * scale, numer_imag / root * scale])


def solution(mesh):
    in_specs = (
        P(("groups", "read", "pair"), "freq", None),
        P("groups", None, None),
        P("groups"),
        P("groups"),
        P("groups", None),
        P("groups"),
        P("groups"),
    )
    out_specs = P(None, ("groups", "read", "pair"), "freq")
    return jax.shard_map(
        per_device, mesh=mesh, in_specs=in_specs, out_specs=out_specs, check_vma=False
    )
```

profile of v0, /device:TPU:0, one launch (start us, length us, event | category | flops | bytes accessed | tf_op | source)
XLA Modules:
  0.0 307.3 jit_solution(17262272560458219443)
XLA Ops:
  7.4 4.9 %collective-permute-start = (f32[1,1,2048]{2,1,0:T(1,128)S(1)}, f32[1,1,2048]{2,1,0:T(1,128)S(1)}, u32[]{:S(2)}, u32[]{:S(2)}) collective-permute-start(f32[1,1,2048]{2,1,0:T(1,128)S(1)} %get-tuple-element.17), channel_id=1, source_target_pairs={{0,4},{4,8},{8,12},{1,5},{5,9},{9,13},{2,6},{6,10},{10,14},{3,7},{... | collective-permute-start | bytes 24584 | tf_op jit(solution)/shard_map/ppermute | solution.py:18
  13.7 8.0 %fusion.260 = (f32[1,512,2047]{2,1,0:T(8,128)}, f32[1,512,2047]{2,1,0:T(8,128)}) fusion(f32[1,512,2048]{2,1,0:T(8,128)} %param.7), kind=kLoop, calls=%fused_computation.295 | loop fusion | bytes 16769024 | tf_op jit(solution)/shard_map/slice | solution.py:125
  22.4 1.3 fusion.152
  23.7 1.3 fusion.151
  25.1 9.5 %fusion.6 = f32[64,8,16,128]{3,1,2,0:T(8,128)S(1)} fusion(f32[1,512,2048]{2,1,0:T(8,128)} %param.7, f32[1,1,2048]{2,1,0:T(1,128)S(1)} %collective-permute-done.1, f32[1,1,2048]{2,1,0:T(1,128)S(1)} %collective-permute-done, f32[1,512,2047]{2,1,0:T(8,128)} %get-tuple-element.16, f32[1,512,2047]{2,1,0:T(8,128)} %get-tuple-element.15, pred[512]{0:T(512)(128)(4,1)S(1)} %fusion.151), kind=kLoop, calls=%fused_computation.7 | loop fusion | flops 8388608 | bytes 16790016
  35.5 4.0 %fusion.119 = f32[16,512,128]{2,0,1:T(8,128)S(1)} fusion(f32[512,16,128]{2,1,0:T(8,128)S(1)} %bitcast.210), kind=kOutput, calls=%fused_computation.151 | convolution fusion | flops 201330176 | bytes 8388608 | tf_op jit(solution)/shard_map/...ab,ad->...db/dot_general | solution.py:41
  39.5 4.8 %fusion.8 = (f32[512,16,128]{2,1,0:T(8,128)S(1)}, f32[512,16,128]{2,1,0:T(8,128)S(1)}) fusion(f32[16,512,128]{2,0,1:T(8,128)S(1)} %fusion.119, f32[16,128]{1,0:T(8,128)S(1)} %get-tuple-element.23, f32[16,128]{1,0:T(8,128)S(1)} %get-tuple-element.24, f32[512,16,128]{2,1,0:T(8,128)S(1)} %bitcast.211), kind=kOutput, calls=%fused_computation.14 | convolution fusion | flops 208670208 | bytes 16793600 | tf_op jit(solution)/shard_map/...ab,ad->...db/dot_general | solution.py:40
  44.3 5.9 %fusion.13 = f32[128,512,16]{1,0,2:T(8,128)S(1)} fusion(f32[512,16,128]{2,1,0:T(8,128)S(1)} %get-tuple-element.8), kind=kOutput, calls=%fused_computation.23 | convolution fusion | flops 1610842112 | bytes 8388608 | tf_op jit(solution)/shard_map/...db,bc->...cd/dot_general | solution.py:54
  50.2 5.4 %fusion.11 = f32[128,512,16]{1,0,2:T(8,128)S(1)} fusion(f32[512,16,128]{2,1,0:T(8,128)S(1)} %get-tuple-element.8), kind=kOutput, calls=%fused_computation.21 | convolution fusion | flops 1610842112 | bytes 8388608 | tf_op jit(solution)/shard_map/...db,bc->...cd/dot_general | solution.py:57
  55.6 6.0 %add_bitcast_fusion = f32[1,512,128,16]{1,2,3,0:T(8,128)S(1)} fusion(f32[128,512,16]{1,0,2:T(8,128)S(1)} %fusion.13, f32[512,16,128]{2,1,0:T(8,128)S(1)} %get-tuple-element.7), kind=kOutput, calls=%fused_computation.20 | convolution fusion | flops 1611890688 | bytes 12582912 | tf_op jit(solution)/shard_map/...db,bc->...cd/dot_general | solution.py:54
  61.6 2.4 copy.70
  64.3 5.9 %subtract_bitcast_fusion = f32[1,512,128,16]{1,2,3,0:T(8,128)S(1)} fusion(f32[128,512,16]{1,0,2:T(8,128)S(1)} %fusion.11, f32[512,16,128]{2,1,0:T(8,128)S(1)} %get-tuple-element.7), kind=kOutput, calls=%fused_computation.19 | convolution fusion | flops 1611890688 | bytes 12582912 | tf_op jit(solution)/shard_map/...db,bc->...cd/dot_general | solution.py:57
  70.1 2.8 copy.73
  73.7 2.7 copy.74
  76.4 6.1 %all-to-all-start = ((f32[512,1,4,512]{0,3,1,2:T(8,128)}), f32[512,1,4,512]{0,3,1,2:T(8,128)}, u32[]{:S(2)}, u32[]{:S(2)}) async-start(f32[512,1,4,512]{0,3,1,2:T(8,128)} %bitcast.212), calls=%async_computation | async-start | bytes 8388608 | tf_op jit(solution)/shard_map/all_to_all | solution.py:140
  83.3 1.3 multiply_divide_fusion
  85.2 5.7 %fusion.61 = f32[256,2048]{1,0:T(8,128)S(1)} fusion(f32[16,256]{1,0:T(8,128)S(1)} %fusion.129, s32[16]{0:T(128)S(1)} %and_select_fusion), kind=kOutput, calls=%fused_computation.88 | convolution fusion | flops 101122048 | bytes 2113600 | tf_op jit(solution)/shard_map/ma,nap->nmp/dot_general | solution.py:92
  90.8 7.2 %fusion.59 = f32[256,2048]{1,0:T(8,128)} fusion(f32[16,256]{1,0:T(8,128)S(1)} %convolution_negate_fusion.1, s32[16]{0:T(128)S(1)} %and_select_fusion), kind=kOutput, calls=%fused_computation.87 | convolution fusion | flops 101122048 | bytes 2113600 | tf_op jit(solution)/shard_map/ma,nap->nmp/dot_general | solution.py:95
  98.1 7.8 %fusion.22 = f32[2048,256]{0,1:T(8,128)} fusion(f32[256,2048]{1,0:T(8,128)S(1)} %fusion.61, f32[16,256]{1,0:T(8,128)S(1)} %convolution_negate_fusion.1, f32[]{:T(128)} %get-tuple-element.22, s32[16]{0:T(128)S(1)} %and_select_fusion), kind=kOutput, calls=%fused_computation.34 | convolution fusion | flops 102170624 | bytes 4210756 | tf_op jit(solution)/shard_map/ma,nap->nmp/dot_general | solution.py:92
  105.9 69.5 %all-to-all-done = f32[512,1,4,512]{0,3,1,2:T(8,128)} async-done(((f32[512,1,4,512]{0,3,1,2:T(8,128)}), f32[512,1,4,512]{0,3,1,2:T(8,128)}, u32[]{:S(2)}, u32[]{:S(2)}) %all-to-all-start) | async-done | bytes 4194336 | tf_op jit(solution)/shard_map/all_to_all | solution.py:140
  175.4 5.3 %copy.76 = f32[4,512,1,1,512]{4,1,0,3,2:T(8,128)} copy(f32[4,512,1,1,512]{1,4,0,3,2:T(8,128)} %bitcast.25) | data formatting | bytes 8388608 | tf_op jit(solution)/shard_map/all_to_all | solution.py:140
  180.6 5.9 %reshape.291 = f32[2048,1,2,256]{3,2,0,1:T(2,128)} reshape(f32[4,512,1,1,512]{4,1,0,3,2:T(8,128)} %copy.76) | data formatting | bytes 8388608 | tf_op jit(solution)/shard_map/reshape | solution.py:141
  186.5 7.6 %slice_bitcast_fusion = (f32[1,256,2048]{1,0,2:T(1,128)}, f32[1,256,2048]{1,0,2:T(1,128)S(1)}) fusion(f32[2048,1,2,256]{3,2,0,1:T(2,128)} %reshape.291), kind=kLoop, calls=%fused_computation.35 | loop fusion | bytes 8388608 | tf_op jit(solution)/shard_map/transpose | solution.py:143
  194.1 1.5 copy.93
  195.6 2.2 copy.91
  197.8 3.3 %fusion.116 = f32[16,256,128]{2,0,1:T(8,128)} fusion(f32[256,16,128]{2,1,0:T(8,128)S(1)} %copy.91), kind=kOutput, calls=%fused_computation.148 | convolution fusion | flops 100666880 | bytes 4194304 | tf_op jit(solution)/shard_map/...ab,ad->...db/dot_general | solution.py:41
  201.1 3.3 %fusion.122 = f32[16,256,128]{2,0,1:T(8,128)} fusion(f32[256,16,128]{2,1,0:T(8,128)S(1)} %copy.91), kind=kOutput, calls=%fused_computation.154 | convolution fusion | flops 100666880 | bytes 4194304 | tf_op jit(solution)/shard_map/...ab,ad->...db/dot_general | solution.py:40
  204.4 1.4 copy.94
  205.8 2.5 copy.92
  209.6 3.8 %negate_add_fusion = f32[16,256,128]{2,0,1:T(8,128)S(1)} fusion(f32[16,256,128]{2,0,1:T(8,128)} %fusion.116, f32[256,16,128]{2,1,0:T(8,128)S(1)} %copy.92), kind=kOutput, calls=%fused_computation.55 | convolution fusion | flops 101715456 | bytes 6291456 | tf_op jit(solution)/shard_map/...ab,ad->...db/dot_general | solution.py:45
  213.4 4.0 %fusion.31 = (f32[256,16,128]{2,1,0:T(8,128)S(1)}, f32[256,16,128]{2,1,0:T(8,128)S(1)}) fusion(f32[16,256,128]{2,0,1:T(8,128)S(1)} %negate_add_fusion, f32[16,128]{1,0:T(8,128)S(1)} %get-tuple-element.23, f32[16,128]{1,0:T(8,128)S(1)} %get-tuple-element.24, f32[16,256,128]{2,0,1:T(8,128)S(1)} %copy-done.2, f32[256,16,128]{2,1,0:T(8,128)} %copy-done), kind=kOutput, calls=%fused_computation.48 | convolution fusion | flops 104336896 | bytes 10502144 | tf_op jit(solution)/shard_map/...ab,ad->...db/dot_general | solution.py:44
  217.4 2.6 fusion.36
  220.0 3.9 %fusion.34 = f32[128,256,16]{1,0,2:T(8,128)} fusion(f32[256,16,128]{2,1,0:T(8,128)S(1)} %get-tuple-element.12), kind=kOutput, calls=%fused_computation.56 | convolution fusion | flops 805535744 | bytes 4194304 | tf_op jit(solution)/shard_map/...db,bc->...cd/dot_general | solution.py:57
  223.9 3.0 add_bitcast_fusion.1
  226.9 2.5 copy.81
  229.5 2.9 copy.82
  232.4 4.2 %subtract_bitcast_fusion.1 = f32[1,256,128,16]{1,2,3,0:T(8,128)S(1)} fusion(f32[128,256,16]{1,0,2:T(8,128)} %fusion.34, f32[256,16,128]{2,1,0:T(8,128)S(1)} %get-tuple-element.11), kind=kOutput, calls=%fused_computation.53 | convolution fusion | flops 806060032 | bytes 6291456 | tf_op jit(solution)/shard_map/...db,bc->...cd/dot_general | solution.py:57
  236.6 2.5 copy.85
  239.2 3.1 %copy.86 = f32[256,2048]{1,0:T(8,128)} copy(f32[256,2048]{0,1:T(8,128)} %bitcast.218) | data formatting | bytes 4194304 | tf_op jit(solution)/shard_map/reshape.71
  242.3 9.0 %fusion.28 = (f32[2048,256]{0,1:T(8,128)S(1)}, f32[2048,256]{0,1:T(8,128)S(1)}) fusion(f32[256,2048]{1,0:T(8,128)} %copy.86, f32[2048,256]{0,1:T(8,128)} %fusion.22, f32[256,2048]{1,0:T(8,128)S(1)} %copy-done.1, f32[256,2048]{1,0:T(8,128)} %fusion.59, f32[16,256]{1,0:T(8,128)S(1)} %fusion.129, s32[16]{0:T(128)S(1)} %and_select_fusion, f32[]{:T(128)} %get-tuple-element.22), kind=kOutput, calls=%fused_computation.41 | convolution fusion | flops 105316352 | bytes 12599364 | tf_op jit(solution)/shard_map/ma,nap->nmp/dot_general | solution.py:95
  251.3 2.4 pad_maximum_fusion.3
  254.5 2.0 fusion.83
  256.4 2.0 fusion.85
  258.4 2.0 fusion.87
  260.3 2.5 fusion.27
  262.9 34.6 %reduce-scatter.2.cloned.1.call-done = f32[512,512]{0,1:T(8,128)} async-done(((f32[2048,512]{0,1:T(8,128)}), f32[512,512]{0,1:T(8,128)}) %reduce-scatter.2.cloned.1.call-update) | async-done | bytes 1048592 | tf_op jit(solution)/shard_map/reduce_scatter | solution.py:155
  297.5 1.4 fusion.56
  299.0 1.3 copy.87
  (42 shorter events, 8.1 us)
Async XLA Ops:
  7.4 17.6 %collective-permute-start = (f32[1,1,2048]{2,1,0:T(1,128)S(1)}, f32[1,1,2048]{2,1,0:T(1,128)S(1)}, u32[]{:S(2)}, u32[]{:S(2)}) collective-permute-start(f32[1,1,2048]{2,1,0:T(1,128)S(1)} %get-tuple-element.17), channel_id=1, source_target_pairs={{0,4},{4,8},{8,12},{1,5},{5,9},{9,13},{2,6},{6,10},{10,14},{3,7},{... | collective-permute-start | bytes 24584 | tf_op jit(solution)/shard_map/ppermute | solution.py:18
  12.4 12.7 %collective-permute-start.1 = (f32[1,1,2048]{2,1,0:T(1,128)S(1)}, f32[1,1,2048]{2,1,0:T(1,128)S(1)}, u32[]{:S(2)}, u32[]{:S(2)}) collective-permute-start(f32[1,1,2048]{2,1,0:T(1,128)S(1)} %get-tuple-element.18), channel_id=1, source_target_pairs={{4,0},{8,4},{12,8},{5,1},{9,5},{13,9},{6,2},{10,6},{14,10},{7,3},{... | collective-permute-start | bytes 24584 | tf_op jit(solution)/shard_map/ppermute | solution.py:21
  13.7 8.1 %copy-start.9 = (s32[4]{0:T(128)S(1)}, s32[4]{0:T(128)}, u32[]{:S(2)}) copy-start(s32[4]{0:T(128)} %param.13) | copy-start | bytes 52
  13.7 8.7 %copy-start.5 = (s32[4,2]{0,1:T(2,128)S(1)}, s32[4,2]{0,1:T(2,128)}, u32[]{:S(2)}) copy-start(s32[4,2]{0,1:T(2,128)} %param.11) | copy-start | bytes 100
  76.4 6.8 %copy-start.4 = (f32[4,16,16]{2,1,0:T(8,128)S(1)}, f32[4,16,16]{2,1,0:T(8,128)}, u32[]{:S(2)}) copy-start(f32[4,16,16]{2,1,0:T(8,128)} %param.8) | copy-start | bytes 12292
  76.4 6.9 %copy-start.6 = (f32[4]{0:T(128)S(1)}, f32[4]{0:T(128)}, u32[]{:S(2)}) copy-start(f32[4]{0:T(128)} %param.10) | copy-start | bytes 52
  76.4 6.9 %copy-start.7 = (f32[4]{0:T(128)S(1)}, f32[4]{0:T(128)}, u32[]{:S(2)}) copy-start(f32[4]{0:T(128)} %param.9) | copy-start | bytes 52
  76.4 6.9 %copy-start.8 = (s32[4]{0:T(128)S(1)}, s32[4]{0:T(128)}, u32[]{:S(2)}) copy-start(s32[4]{0:T(128)} %param.12) | copy-start | bytes 52
  76.4 99.0 %all-to-all-start = ((f32[512,1,4,512]{0,3,1,2:T(8,128)}), f32[512,1,4,512]{0,3,1,2:T(8,128)}, u32[]{:S(2)}, u32[]{:S(2)}) async-start(f32[512,1,4,512]{0,3,1,2:T(8,128)} %bitcast.212), calls=%async_computation | async-start | bytes 8388608 | tf_op jit(solution)/shard_map/all_to_all | solution.py:140
  82.5 215.0 %reduce-scatter.2.cloned.1.call-start = ((), (), s32[]{:S(2)}) async-start(), calls=%async_computation.2 | async-start | bytes 5242880 | tf_op jit(solution)/shard_map/reduce_scatter | solution.py:155
  201.1 3.3 %copy-start.3 = (f32[1,256,2048]{1,0,2:T(1,128)S(1)}, f32[1,256,2048]{1,0,2:T(1,128)}, u32[]{:S(2)}) copy-start(f32[1,256,2048]{1,0,2:T(1,128)} %get-tuple-element.13) | copy-start | bytes 6291460
  208.3 1.3 copy-start
  209.6 3.8 %copy-start.2 = (f32[16,256,128]{2,0,1:T(8,128)S(1)}, f32[16,256,128]{2,0,1:T(8,128)}, u32[]{:S(2)}) copy-start(f32[16,256,128]{2,0,1:T(8,128)} %fusion.122) | copy-start | bytes 6291460
  239.2 3.1 %copy-start.1 = (f32[256,2048]{1,0:T(8,128)S(1)}, f32[256,2048]{1,0:T(8,128)}, u32[]{:S(2)}) copy-start(f32[256,2048]{1,0:T(8,128)} %copy.82) | copy-start | bytes 6291460
Sparse Core Ops, SparseCore 0:
  253.9 43.5 reduce-scatter.1
where the time goes:
time: 311 us; the launch traced here: 307 us
  waiting for transfers between devices  104 us (33%)
  matrix products  99.4 us (32%)
  local copies, waits for them, and re-layouts  58.2 us (19%)
  other arithmetic  19.3 us (6%)
  between operations  14 us (5%)
  starting transfers between devices  12.3 us (4%)
    all_to_all x1, waiting for transfers between devices, per_device(): lax.all_to_all(spectra, 'freq', split_axis=2, concat_axis=0, tiled=True)  69.5 us
    reduce_scatter x1, waiting for transfers between devices, per_device(): lax.psum_scatter(jnp.concatenate([term_real, term_imag], axis=1), ('read'...  34.6 us
    dot_general x2, matrix products, psf_spectrum(): jnp.einsum('ma,nap->nmp', sin_u, q_real, precision=HIGHEST)  11.5 us
    another operation x4, local copies, waits for them, and re-layouts  10.7 us
    dot_general x2, matrix products, fourier(): jnp.einsum('...db,bc->...cd', mid_re, sin_b, precision=HIGHEST)  10.1 us
    dot_general x2, matrix products, psf_spectrum(): jnp.einsum('ma,nap->nmp', sin_u, q_imag, precision=HIGHEST)  9.76 us
    unnamed x1, other arithmetic  9.49 us
    dot_general x2, matrix products, fourier(): jnp.einsum('...db,bc->...cd', mid_im, cos_b, precision=HIGHEST)  9.32 us
  transfers between devices with their start and end apart: 4, of which 2 were waited for; matrix products, arithmetic and copies ran while one was open for 14% of the time, Pallas kernels for 0%

commit v1 on v0

v1 whole, which is shorter than its diff:
```python
import functools
import math

import jax
import jax.numpy as jnp
import ml_dtypes
import numpy as np
from jax import lax
from jax.experimental import pallas as pl
from jax.experimental.pallas import tpu as pltpu
from jax.sharding import PartitionSpec as P

HIGHEST = lax.Precision.HIGHEST
TWO_PI = 2.0 * math.pi
HALO = 16
TILE = 128
BF16 = jnp.bfloat16
F32 = jnp.float32
READERS = ("read", "pair")


def split_np(table):
    hi = table.astype(np.float32).astype(ml_dtypes.bfloat16)
    lo = (table - hi.astype(np.float64)).astype(np.float32).astype(ml_dtypes.bfloat16)
    return hi, lo


def split(value):
    hi = value.astype(BF16)
    return hi, (value - hi.astype(F32)).astype(BF16)


def angles(left, right, modulus):
    return (np.outer(left, right) % modulus).astype(np.float64) * (TWO_PI / modulus)


def dot(left, right):
    return jnp.dot(left, right, preferred_element_type=F32)


def column_order(width, freqs, readers):
    share = width // 2 // freqs // readers
    parity = np.arange(2)[:, None, None, None]
    reader = np.arange(readers)[None, :, None, None]
    freq = np.arange(freqs)[None, None, :, None]
    inner = np.arange(share // 2)[None, None, None, :]
    ids = freq * (share * readers) + reader * share + 2 * inner + parity
    return ids.reshape(2, -1, TILE)


def row_tables(ids, width):
    half = np.arange(width // 2)
    parts = []
    for tile in range(ids.shape[1]):
        both = []
        for parity in range(2):
            phase = angles(half, ids[parity, tile], width)
            both.append(np.concatenate([np.cos(phase), -np.sin(phase)], axis=1))
        parts.append(np.stack(both))
    return split_np(np.stack(parts))


def front_kernel(info, low, block, high, taps, th, tl, out, ext, ch, cl, grid):
    rows, width = block.shape
    half = width // 2
    height = info[3]

    @pl.when(pl.program_id(0) == 0)
    def _():
        ext[:HALO] = low[...]
        ext[HALO : HALO + rows] = block[...]
        ext[HALO + rows :] = high[...]
        cols = lax.broadcasted_iota(jnp.int32, (16, width), 1)

        def clean(i, carry):
            at = pl.multiple_of(i * 16, 16)
            piece = ext[pl.ds(at, 32), :]
            mid = piece[8:24]
            ids = info[0] - 8 + at + lax.broadcasted_iota(jnp.int32, (16, 1), 0)
            ids = jnp.where(ids < 0, ids + height, ids)
            ids = jnp.where(ids >= height, ids - height, ids)
            up = jnp.where(ids == 0, 0.0, piece[7:23])
            down = jnp.where(ids == height - 1, 0.0, piece[9:25])
            left = jnp.where(cols == 0, 0.0, pltpu.roll(mid, 1, 1))
            right = jnp.where(cols == width - 1, 0.0, pltpu.roll(mid, width - 1, 1))
            inside = (ids >= info[1]) & (ids < info[2])
            cell = jnp.where(inside, mid - 0.25 * (up + down + left + right), 0.0)
            for parity in range(2):
                if parity == 0:
                    fold = cell[:, :half] + cell[:, half:]
                else:
                    fold = cell[:, :half] - cell[:, half:]
                hi, lo = split(fold)
                ch[parity, pl.ds(at, 16), :] = hi
                cl[parity, pl.ds(at, 16), :] = lo
            return carry

        lax.fori_loop(0, (rows + 16) // 16, clean, 0)

    for parity in range(2):
        grid[parity] = (
            dot(ch[parity], th[0, parity])
            + dot(ch[parity], tl[0, parity])
            + dot(cl[parity], th[0, parity])
        )

    def fir(i, carry):
        at = pl.multiple_of(i * 32, 32)
        for parity in range(2):
            re = grid[parity, pl.ds(at, 48), :TILE]
            im = grid[parity, pl.ds(at, 48), TILE:]
            sum_re = jnp.zeros((32, TILE), F32)
            sum_im = jnp.zeros((32, TILE), F32)
            for k in range(8):
                shift_re = re[k : k + 40]
                shift_im = im[k : k + 40]
                for a in (k, k + 8):
                    qr = taps[0, parity, 0, a : a + 1, :]
                    qi = taps[0, parity, 1, a : a + 1, :]
                    xr = shift_re[a - k : a - k + 32]
                    xi = shift_im[a - k : a - k + 32]
                    sum_re = sum_re + (qr * xr + qi * xi)
                    sum_im = sum_im + (qr * xi - qi * xr)
            lane = parity * 2 * TILE
            out[0, pl.ds(at, 32), lane : lane + TILE] = sum_re
            out[0, pl.ds(at, 32), lane + TILE : lane + 2 * TILE] = sum_im
        return carry

    lax.fori_loop(0, rows // 32, fir, 0)


def front(info, low, block, high, taps, tables):
    rows, width = block.shape
    tiles = tables[0].shape[0]
    whole = lambda shape: pl.BlockSpec(shape, lambda t: (0,) * len(shape))
    table_spec = pl.BlockSpec((1, 2, width // 2, 2 * TILE), lambda t: (t, 0, 0, 0))
    return pl.pallas_call(
        front_kernel,
        grid=(tiles,),
        out_shape=jax.ShapeDtypeStruct((tiles, rows, 4 * TILE), F32),
        in_specs=[
            pl.BlockSpec(memory_space=pltpu.SMEM),
            whole((HALO, width)),
            whole((rows, width)),
            whole((HALO, width)),
            pl.BlockSpec((1, 2, 2, taps.shape[3], TILE), lambda t: (t, 0, 0, 0, 0)),
            table_spec,
            table_spec,
        ],
        out_specs=pl.BlockSpec((1, rows, 4 * TILE), lambda t: (t, 0, 0)),
        scratch_shapes=[
            pltpu.VMEM((rows + 2 * HALO, width), F32),
            pltpu.VMEM((2, rows + 16, width // 2), BF16),
            pltpu.VMEM((2, rows + 16, width // 2), BF16),
            pltpu.VMEM((2, rows + 16, 2 * TILE), F32),
        ],
        compiler_params=pltpu.CompilerParams(vmem_limit_bytes=48 * 1024 * 1024),
        name="front",
    )(info, low, block, high, taps, *tables)


def column_tables(height):
    quarter = height // 4
    inner = np.arange(quarter)
    parts = []
    for j in range(4):
        phase = angles(4 * np.arange(quarter) + j, inner, height)
        parts.append(np.concatenate([np.cos(phase), np.sin(phase)], axis=1))
    return split_np(np.stack(parts))


def order_matrix(share):
    size = 2 * share
    table = np.zeros((size, 2 * size), np.float32)
    for part in range(2):
        for parity in range(2):
            for j in range(share // 2):
                source = part * share + parity * (share // 2) + j
                place = 2 * j + parity
                table[source, part * share + place] = 1.0
                table[source, size + (1 - part) * share + place] = -1.0 if part == 0 else 1.0
    return table.astype(ml_dtypes.bfloat16)


def column_kernel(x, order, th, tl, out):
    height, lanes = x.shape
    quarter = height // 4
    step = pl.program_id(0)
    for j in range(4):

        @pl.when(step == j)
        def _(j=j):
            parts = []
            for f in range(4):
                hi, lo = split(x[f * quarter : (f + 1) * quarter])
                parts.append(dot(hi, order[...]) + dot(lo, order[...]))
            if j % 2 == 0:
                even, odd = parts[0] + parts[2], parts[1] + parts[3]
                mix = even + odd if j == 0 else even - odd
                top, low = mix[:, :lanes], mix[:, lanes:]
            else:
                even, odd = parts[0] - parts[2], parts[1] - parts[3]
                sign = 1.0 if j == 1 else -1.0
                top = even[:, :lanes] + sign * odd[:, lanes:]
                low = even[:, lanes:] - sign * odd[:, :lanes]
            both = jnp.concatenate([top, low], axis=0)
            hi, lo = split(both)
            wide = dot(th[0], jnp.concatenate([hi, lo], axis=1))
            result = wide[:, :lanes] + wide[:, lanes:] + dot(tl[0], hi)
            out[pl.ds(j, quarter, stride=4), :] = result


def columns(x, order, tables):
    height, lanes = x.shape
    quarter = height // 4
    table_spec = pl.BlockSpec((1, quarter, 2 * quarter), lambda j: (j, 0, 0))
    return pl.pallas_call(
        column_kernel,
        grid=(4,),
        out_shape=jax.ShapeDtypeStruct((height, lanes), F32),
        in_specs=[
            pl.BlockSpec((height, lanes), lambda j: (0, 0)),
            pl.BlockSpec((lanes, 2 * lanes), lambda j: (0, 0)),
            table_spec,
            table_spec,
        ],
        out_specs=pl.BlockSpec((height, lanes), lambda j: (0, 0)),
        compiler_params=pltpu.CompilerParams(vmem_limit_bytes=48 * 1024 * 1024),
        name="columns",
    )(x, order, *tables)


def denom_kernel(weight, rows, cols, out):
    count = cols.shape[0]
    lanes = out.shape[1]
    total = jnp.zeros(out.shape, F32)
    rh, rl = split(rows[...])
    for e in range(count):
        chh, cll = split(cols[e])
        psf = dot(rh, chh) + dot(rh, cll) + dot(rl, chh)
        total = total + weight[e] * (psf[:, :lanes] * psf[:, :lanes] + psf[:, lanes:] * psf[:, lanes:])
    out[...] = lax.rsqrt(total)


def per_device(exposures, stamps, zero_point, noise_var, footprint, accept, assign):
    exp_dev, rows_dev, width = exposures.shape
    freqs = lax.axis_size("freq")
    readers = lax.axis_size(READERS)
    height = rows_dev * freqs
    per_freq = width // 2 // freqs
    share = per_freq // readers
    out_rows = height // readers
    stamp_len = stamps.shape[1]
    count_all = assign.shape[0]
    freq_at = lax.axis_index("freq")
    reader_at = lax.axis_index(READERS)
    ids = column_order(width, freqs, readers)
    tiles = ids.shape[1]
    offsets = np.arange(stamp_len) - stamp_len // 2

    block = exposures[0]
    forward = [(i, (i + 1) % freqs) for i in range(freqs)]
    backward = [(t, s) for s, t in forward]
    low = lax.ppermute(block[rows_dev - HALO :], "freq", forward)
    high = lax.ppermute(block[:HALO], "freq", backward)

    labels = jnp.arange(count_all, dtype=jnp.int32)
    owner = jnp.sum(jnp.where(labels == reader_at, assign, 0))
    chosen = labels == owner
    low_row = jnp.sum(jnp.where(chosen, footprint[:, 0], 0))
    high_row = jnp.sum(jnp.where(chosen, footprint[:, 1], 0))
    accepted = accept.astype(F32)
    numer_weight = accepted * zero_point / noise_var
    denom_weight = accepted * zero_point * zero_point / noise_var
    scale = 1.0 / math.sqrt(height * width)
    weight = jnp.sum(jnp.where(chosen, numer_weight, 0.0)) * scale
    stamp = jnp.sum(jnp.where(chosen[:, None, None], stamps, 0.0), axis=0) * weight
    tap_phase = angles(offsets, ids.reshape(-1), width)
    tap_table = np.stack([np.cos(tap_phase), -np.sin(tap_phase)]).astype(np.float32)
    taps = jnp.einsum("ab,cbp->cap", stamp, tap_table, precision=HIGHEST)
    taps = taps.reshape(2, stamp_len, 2, tiles, TILE).transpose(3, 2, 0, 1, 4)
    info = jnp.stack([freq_at * rows_dev, low_row, high_row, jnp.int32(height)]).astype(jnp.int32)

    terms = front(info, low, block, high, taps, row_tables(ids, width))
    if tiles != readers:
        terms = terms.reshape(tiles, rows_dev, 2, 2, readers // tiles, TILE * tiles // readers)
        terms = terms.transpose(0, 4, 1, 2, 3, 5).reshape(readers, rows_dev, -1)
    summed = lax.psum_scatter(terms, READERS, scatter_dimension=0, tiled=True)
    summed = summed.reshape(rows_dev, 2, 2, freqs, share // 2)
    summed = summed.transpose(3, 0, 2, 1, 4).reshape(freqs, rows_dev, 2 * share)
    gathered = lax.all_to_all(summed, "freq", split_axis=0, concat_axis=0, tiled=True)
    grid = columns(gathered.reshape(height, 2 * share), order_matrix(share), column_tables(height))
    grid = lax.all_to_all(
        grid.reshape(readers, out_rows, 2 * share), READERS, split_axis=0, concat_axis=0, tiled=True
    )
    numer = grid.reshape(readers, out_rows, 2, share).transpose(2, 1, 0, 3)
    numer = numer.reshape(2, out_rows, per_freq)

    all_u = angles(np.arange(height), offsets, height)
    all_rows = np.concatenate([np.cos(all_u), np.sin(all_u)], axis=1).astype(np.float32)
    psf_rows = lax.dynamic_slice_in_dim(jnp.asarray(all_rows), reader_at * out_rows, out_rows, 0)
    all_v = angles(offsets, np.arange(width // 2), width)
    all_cols = np.stack([np.cos(all_v), -np.sin(all_v)]).astype(np.float32)
    own_cols = lax.dynamic_slice_in_dim(jnp.asarray(all_cols), freq_at * per_freq, per_freq, 2)
    q = jnp.einsum("nab,cbp->cnap", stamps, own_cols, precision=HIGHEST)
    psf_cols = jnp.concatenate(
        [jnp.concatenate([q[0], q[1]], axis=2), jnp.concatenate([q[1], -q[0]], axis=2)], axis=1
    )
    inverse = pl.pallas_call(
        denom_kernel,
        out_shape=jax.ShapeDtypeStruct((out_rows, per_freq), F32),
        in_specs=[
            pl.BlockSpec(memory_space=pltpu.SMEM),
            pl.BlockSpec(memory_space=pltpu.VMEM),
            pl.BlockSpec(memory_space=pltpu.VMEM),
        ],
        out_specs=pl.BlockSpec(memory_space=pltpu.VMEM),
        compiler_params=pltpu.CompilerParams(vmem_limit_bytes=32 * 1024 * 1024),
        name="denom",
    )(denom_weight, psf_rows, psf_cols)
    return numer * inverse


def solution(mesh):
    in_specs = (
        P(("groups", "read", "pair"), "freq", None),
        P("groups", None, None),
        P("groups"),
        P("groups"),
        P("groups", None),
        P("groups"),
        P("groups"),
    )
    out_specs = P(None, ("groups", "read", "pair"), "freq")
    return jax.shard_map(
        per_device, mesh=mesh, in_specs=in_specs, out_specs=out_specs, check_vma=False
    )
```

time: 311 us -> 170 us (0.55); the launches traced: 307 us -> 170 us
  matrix products: 99.4 us -> 2.17 us
  local copies, waits for them, and re-layouts: 58.2 us -> 9.81 us
  Pallas kernels: 0 us -> 42 us
  waiting for transfers between devices: 104 us -> 79.8 us
  other arithmetic: 19.3 us -> 8.43 us
    dot_general x26 -> x2, matrix products: 99.4 us -> 2.17 us  [the longest x1 1.16 us: per_device(): taps = jnp.einsum('ab,cbp->cap', stamp, tap_table, precision=HIGHEST)]
    pallas_call x0 -> x3, Pallas kernels: none -> 42 us  [the longest x1 31.5 us: front(): pl.pallas_call(front_kernel, grid=(tiles,), out_shape=jax.ShapeDtypeStruc...]
    all_to_all x1 -> x2, waiting for transfers between devices: 69.5 us -> 35.6 us  [the longest x1 24.8 us: per_device(): lax.all_to_all(summed, 'freq', split_axis=0, concat_axis=0, tiled=True)]
    another operation x6 -> x0, local copies, waits for them, and re-layouts: 14.7 us -> none
    reduce_scatter x1, waiting for transfers between devices: 34.6 us -> 44.3 us  [per_device(): summed = lax.psum_scatter(terms, READERS, scatter_dimension=0, tiled=True)]
    unnamed x1 -> x0, other arithmetic: 9.49 us -> none
    slice x4 -> x1, local copies, waits for them, and re-layouts: 9.2 us -> 0.99 us  [per_device(): high = lax.ppermute(block[:HALO], 'freq', backward)]
    transpose x1 -> x2, local copies, waits for them, and re-layouts: 7.57 us -> 1.14 us  [the longest x1 1.07 us: per_device(): summed = summed.transpose(3, 0, 2, 1, 4).reshape(freqs, rows_dev, 2 * share)]
  transfers between devices with their start and end apart: 4 -> 5, of which waited for: 2 -> 3; matrix products, arithmetic and copies ran while one was open for 14% -> 7% of each run, Pallas kernels for 0% -> 1%
where the time goes in v1:
time: 170 us
  waiting for transfers between devices  79.8 us (47%)
  Pallas kernels  42 us (25%)
  between operations  14.3 us (8%)
  starting transfers between devices  13.3 us (8%)
  local copies, waits for them, and re-layouts  9.81 us (6%)
  other arithmetic  8.43 us (5%)
  matrix products  2.17 us (1%)
    reduce_scatter x1, waiting for transfers between devices, per_device(): summed = lax.psum_scatter(terms, READERS, scatter_dimension=0, tiled=True)  44.3 us
    pallas_call x1, Pallas kernels, front(): pl.pallas_call(front_kernel, grid=(tiles,), out_shape=jax.ShapeDtypeStruc...  31.5 us
    all_to_all x1, waiting for transfers between devices, per_device(): lax.all_to_all(summed, 'freq', split_axis=0, concat_axis=0, tiled=True)  24.8 us
    all_to_all x1, waiting for transfers between devices, per_device(): lax.all_to_all(grid.reshape(readers, out_rows, 2 * share), READERS, split...  10.8 us
    pallas_call x1, Pallas kernels, columns(): pl.pallas_call(column_kernel, grid=(4,), out_shape=jax.ShapeDtypeStruct((...  8.19 us
    all_to_all x1, starting transfers between devices, per_device(): lax.all_to_all(summed, 'freq', split_axis=0, concat_axis=0, tiled=True)  4.6 us
    all_to_all x1, starting transfers between devices, per_device(): lax.all_to_all(grid.reshape(readers, out_rows, 2 * share), READERS, split...  3.52 us
  transfers between devices with their start and end apart: 5, of which 3 were waited for; matrix products, arithmetic and copies ran while one was open for 7% of the time, Pallas kernels for 1%

profile of v1, /device:TPU:0, one launch (start us, length us, event | category | flops | bytes accessed | tf_op | source)
XLA Modules:
  0.0 169.8 jit_solution(6260453695079311540)
XLA Ops:
  6.5 0.0 reduce-scatter.2.cloned.1.call-start
  6.5 1.0 slice_bitcast_fusion
  7.5 3.1 %collective-permute-start = (f32[16,2048]{1,0:T(8,128)S(1)}, f32[16,2048]{1,0:T(8,128)S(1)}, u32[]{:S(2)}, u32[]{:S(2)}) collective-permute-start(f32[16,2048]{1,0:T(8,128)S(1)} %get-tuple-element.8), channel_id=1, source_target_pairs={{0,4},{4,8},{8,12},{12,0},{1,5},{5,9},{9,13},{13,1},{2,6},{6,10},{... | collective-permute-start | bytes 393224 | tf_op jit(solution)/shard_map/ppermute | solution.py:264
  10.6 2.1 %collective-permute-start.1 = (f32[16,2048]{1,0:T(8,128)S(1)}, f32[16,2048]{1,0:T(8,128)S(1)}, u32[]{:S(2)}, u32[]{:S(2)}) collective-permute-start(f32[16,2048]{1,0:T(8,128)S(1)} %get-tuple-element.7), channel_id=1, source_target_pairs={{4,0},{8,4},{12,8},{0,12},{5,1},{9,5},{13,9},{1,13},{6,2},{10,6},{... | collective-permute-start | bytes 393224 | tf_op jit(solution)/shard_map/ppermute | solution.py:265
  12.7 1.3 fusion.6
  14.0 0.6 iota_compare_fusion
  14.6 0.8 select_reduce_fusion
  15.5 2.0 %multiply_divide_fusion = (f32[4]{0:T(128)S(1)}, f32[]{:T(128)}) fusion(f32[4]{0:T(128)} %param.18, f32[4]{0:T(128)} %param.17, s32[4]{0:T(128)} %param.20, s32[]{:T(128)} %fusion.6), kind=kLoop, calls=%fused_computation.23 | loop fusion | flops 31 | bytes 72 | tf_op jit(solution)/shard_map/div | solution.py:274
  18.2 1.2 convolution_bitcast_fusion
  19.4 2.1 %fusion.8 = (s32[]{:T(128)}, s32[]{:T(128)}) fusion(s32[4,2]{0,1:T(2,128)} %param.19, s32[]{:T(128)} %fusion.6), kind=kLoop, calls=%fused_computation.22 | loop fusion | flops 18 | bytes 44 | tf_op jit(solution)/shard_map/reduce_sum | solution.py:270
  21.5 0.1 reshape.28
  21.6 1.3 pad_add_fusion.info
  22.9 0.0 collective-permute-done.low
  22.9 0.0 collective-permute-done.1.high
  22.9 31.5 %front.1 = f32[4,512,512]{2,1,0:T(8,128)S(1)} custom-call(s32[4]{0:T(128)S(1)} %pad_add_fusion.info, f32[16,2048]{1,0:T(8,128)S(1)} %collective-permute-done.low, f32[512,2048]{1,0:T(8,128)} %bitcast.55, f32[16,2048]{1,0:T(8,128)S(1)} %collective-permute-done.1.high, f32[4,2,2,16,128]{4,3,2,1,0:T(8,128)S(1)} %bitcast.54, ...), custom_call_target="tpu_custom_call" | custom-call | tf_op jit(solution)/shard_map/front/pallas_call | solution.py:137
  54.4 0.0 copy-start
  54.4 1.9 %copy-done = f32[4,512,512]{2,1,0:T(8,128)} copy-done((f32[4,512,512]{2,1,0:T(8,128)}, f32[4,512,512]{2,1,0:T(8,128)S(1)}, u32[]{:S(2)}) %copy-start) | copy-done | bytes 4194328
  56.3 0.0 reduce-scatter.2.cloned.1.call-update
  56.3 0.0 copy-start.1
  56.4 44.3 %reduce-scatter.2.cloned.1.call-done = f32[1,512,512]{2,1,0:T(8,128)} async-done(((f32[4,512,512]{2,1,0:T(8,128)}), f32[1,512,512]{2,1,0:T(8,128)}) %reduce-scatter.2.cloned.1.call-update) | async-done | bytes 1048592 | tf_op jit(solution)/shard_map/reduce_scatter | solution.py:288
  100.6 1.6 copy.19
  102.2 1.1 copy.20
  103.2 4.6 %all-to-all-start = ((f32[4,512,128]{1,2,0:T(8,128)}), f32[4,512,128]{1,2,0:T(8,128)S(1)}, u32[]{:S(2)}, u32[]{:S(2)}) async-start(f32[4,512,128]{1,2,0:T(8,128)} %bitcast.13), calls=%async_computation.1 | async-start | bytes 2097152 | tf_op jit(solution)/shard_map/all_to_all | solution.py:291
  107.8 1.0 constant_dynamic-slice_fusion.rows
  108.8 24.8 %all-to-all-done = f32[4,512,128]{1,2,0:T(8,128)S(1)} async-done(((f32[4,512,128]{1,2,0:T(8,128)}), f32[4,512,128]{1,2,0:T(8,128)S(1)}, u32[]{:S(2)}, u32[]{:S(2)}) %all-to-all-start) | async-done | bytes 1048608 | tf_op jit(solution)/shard_map/all_to_all | solution.py:291
  133.6 0.3 copy.21
  133.9 0.0 copy-done.1
  133.9 8.2 %columns.1 = f32[2048,128]{1,0:T(8,128)S(1)} custom-call(f32[2048,128]{1,0:T(8,128)S(1)} %bitcast.52, bf16[128,256]{1,0:T(8,128)(2,1)S(1)} %copy-done.1, bf16[4,512,1024]{2,1,0:T(8,128)(2,1)} %constant.49.clone.th, bf16[4,512,1024]{2,1,0:T(8,128)(2,1)} %constant.50.clone.tl), custom_call_target="tpu_custom_call" | custom-call | tf_op jit(solution)/shard_map/columns/pallas_call | solution.py:217
  142.1 0.0 copy-start.2
  142.1 1.3 copy.22
  143.4 3.5 %all-to-all-start.1 = ((f32[4,512,128]{1,2,0:T(8,128)}), f32[4,512,128]{1,2,0:T(8,128)S(1)}, u32[]{:S(2)}, u32[]{:S(2)}) async-start(f32[4,512,128]{1,2,0:T(8,128)} %copy.22), calls=%async_computation.2 | async-start | bytes 2097152 | tf_op jit(solution)/shard_map/all_to_all | solution.py:293
  147.0 0.0 copy-done.2
  147.0 1.0 convolution_bitcast_fusion.1
  148.0 2.3 %denom.1 = f32[512,256]{1,0:T(8,128)S(1)} custom-call(f32[4]{0:T(128)S(1)} %get-tuple-element.11.weight, f32[512,32]{1,0:T(8,128)S(1)} %constant_dynamic-slice_fusion.rows, f32[4,32,512]{2,1,0:T(8,128)S(1)} %maximum_maximum_fusion.cols), custom_call_target="tpu_custom_call" | custom-call | tf_op jit(solution)/shard_map/denom/pallas_call | solution.py:309
  150.4 0.2 copy.24
  150.6 10.8 %all-to-all-done.1 = f32[4,512,128]{1,2,0:T(8,128)S(1)} async-done(((f32[4,512,128]{1,2,0:T(8,128)}), f32[4,512,128]{1,2,0:T(8,128)S(1)}, u32[]{:S(2)}, u32[]{:S(2)}) %all-to-all-start.1) | async-done | bytes 1048608 | tf_op jit(solution)/shard_map/all_to_all | solution.py:293
  161.4 0.1 copy.23
  161.5 0.2 bitcast_multiply_fusion
  161.6 1.3 copy.25
  (4 shorter events, 0.1 us)
Async XLA Ops:
  6.5 94.1 %reduce-scatter.2.cloned.1.call-start = ((), (), s32[]{:S(2)}) async-start(), calls=%async_computation.3 | async-start | bytes 5242880 | tf_op jit(solution)/shard_map/reduce_scatter | solution.py:288
  7.5 15.4 %collective-permute-start = (f32[16,2048]{1,0:T(8,128)S(1)}, f32[16,2048]{1,0:T(8,128)S(1)}, u32[]{:S(2)}, u32[]{:S(2)}) collective-permute-start(f32[16,2048]{1,0:T(8,128)S(1)} %get-tuple-element.8), channel_id=1, source_target_pairs={{0,4},{4,8},{8,12},{12,0},{1,5},{5,9},{9,13},{13,1},{2,6},{6,10},{... | collective-permute-start | bytes 393224 | tf_op jit(solution)/shard_map/ppermute | solution.py:264
  10.6 12.3 %collective-permute-start.1 = (f32[16,2048]{1,0:T(8,128)S(1)}, f32[16,2048]{1,0:T(8,128)S(1)}, u32[]{:S(2)}, u32[]{:S(2)}) collective-permute-start(f32[16,2048]{1,0:T(8,128)S(1)} %get-tuple-element.7), channel_id=1, source_target_pairs={{4,0},{8,4},{12,8},{0,12},{5,1},{9,5},{13,9},{1,13},{6,2},{10,6},{... | collective-permute-start | bytes 393224 | tf_op jit(solution)/shard_map/ppermute | solution.py:265
  54.4 1.9 %copy-start = (f32[4,512,512]{2,1,0:T(8,128)}, f32[4,512,512]{2,1,0:T(8,128)S(1)}, u32[]{:S(2)}) copy-start(f32[4,512,512]{2,1,0:T(8,128)S(1)} %front.1) | copy-start | bytes 12582916
  56.3 77.6 %copy-start.1 = (bf16[128,256]{1,0:T(8,128)(2,1)S(1)}, bf16[128,256]{1,0:T(8,128)(2,1)}, u32[]{:S(2)}) copy-start(bf16[128,256]{1,0:T(8,128)(2,1)} %constant.48.clone.order) | copy-start | bytes 196612
  103.2 30.3 %all-to-all-start = ((f32[4,512,128]{1,2,0:T(8,128)}), f32[4,512,128]{1,2,0:T(8,128)S(1)}, u32[]{:S(2)}, u32[]{:S(2)}) async-start(f32[4,512,128]{1,2,0:T(8,128)} %bitcast.13), calls=%async_computation.1 | async-start | bytes 2097152 | tf_op jit(solution)/shard_map/all_to_all | solution.py:291
  142.1 4.8 %copy-start.2 = (f32[4,16,16]{2,1,0:T(8,128)S(1)}, f32[4,16,16]{2,1,0:T(8,128)}, u32[]{:S(2)}) copy-start(f32[4,16,16]{2,1,0:T(8,128)} %param.16) | copy-start | bytes 12292
  143.4 18.0 %all-to-all-start.1 = ((f32[4,512,128]{1,2,0:T(8,128)}), f32[4,512,128]{1,2,0:T(8,128)S(1)}, u32[]{:S(2)}, u32[]{:S(2)}) async-start(f32[4,512,128]{1,2,0:T(8,128)} %copy.22), calls=%async_computation.2 | async-start | bytes 2097152 | tf_op jit(solution)/shard_map/all_to_all | solution.py:293
Sparse Core Ops, SparseCore 0:
  56.5 44.1 reduce-scatter.1

commit v2 on v1

--- a/solution.py
+++ b/solution.py
@@ -159,6 +159,236 @@
     )(info, low, block, high, taps, *tables)
 
 
+CHUNKS = 4
+MESH = pl.DeviceIdType.MESH
+
+
+def clean_rows(info, low, block, high, ext, ch, cl, height):
+    rows, width = block.shape
+    half = width // 2
+    ext[:HALO] = low[...]
+    ext[HALO : HALO + rows] = block[...]
+    ext[HALO + rows :] = high[...]
+    cols = lax.broadcasted_iota(jnp.int32, (16, width), 1)
+
+    def clean(i, carry):
+        at = pl.multiple_of(i * 16, 16)
+        piece = ext[pl.ds(at, 32), :]
+        mid = piece[8:24]
+        ids = info[0] - 8 + at + lax.broadcasted_iota(jnp.int32, (16, 1), 0)
+        ids = jnp.where(ids < 0, ids + height, ids)
+        ids = jnp.where(ids >= height, ids - height, ids)
+        up = jnp.where(ids == 0, 0.0, piece[7:23])
+        down = jnp.where(ids == height - 1, 0.0, piece[9:25])
+        left = jnp.where(cols == 0, 0.0, pltpu.roll(mid, 1, 1))
+        right = jnp.where(cols == width - 1, 0.0, pltpu.roll(mid, width - 1, 1))
+        inside = (ids >= info[1]) & (ids < info[2])
+        cell = jnp.where(inside, mid - 0.25 * (up + down + left + right), 0.0)
+        for parity in range(2):
+            if parity == 0:
+                fold = cell[:, :half] + cell[:, half:]
+            else:
+                fold = cell[:, :half] - cell[:, half:]
+            hi, lo = split(fold)
+            ch[parity, pl.ds(at, 16), :] = hi
+            cl[parity, pl.ds(at, 16), :] = lo
+        return carry
+
+    lax.fori_loop(0, (rows + 16) // 16, clean, 0)
+
+
+def fused_kernel(
+    freqs, info, low, block, high, taps, th, tl, out,
+    ext, ch, cl, grid, bufh, bufl, work, pair_in, read_in, freq_out, freq_in,
+    table_sem, pair_send, pair_recv, read_send, read_recv, freq_send, freq_recv,
+):
+    rows, width = block.shape
+    height = rows * freqs
+    chunk = rows // CHUNKS
+    share = TILE // freqs
+    r = lax.axis_index("read")
+    p = lax.axis_index("pair")
+    f = lax.axis_index("freq")
+
+    def tile_at(s):
+        rd = jnp.where(s < 2, 1 - r, r)
+        pd = jnp.where(s % 2 == 0, 1 - p, p)
+        return rd * 2 + pd
+
+    def table_copies(s):
+        t = tile_at(s)
+        return (
+            pltpu.make_async_copy(th.at[t], bufh.at[s], table_sem.at[0, s]),
+            pltpu.make_async_copy(tl.at[t], bufl.at[s], table_sem.at[1, s]),
+        )
+
+    def pair_copy(n):
+        return pltpu.make_async_remote_copy(
+            src_ref=work.at[2 * n], dst_ref=pair_in.at[n],
+            send_sem=pair_send.at[n], recv_sem=pair_recv.at[n],
+            device_id={"pair": 1 - p}, device_id_type=MESH,
+        )
+
+    def read_copy(c):
+        part = pl.ds(c * chunk, chunk)
+        return pltpu.make_async_remote_copy(
+            src_ref=work.at[1, part], dst_ref=read_in.at[part],
+            send_sem=read_send.at[c], recv_sem=read_recv.at[c],
+            device_id={"read": 1 - r}, device_id_type=MESH,
+        )
+
+    def freq_copy(d, c):
+        part = pl.ds(c * chunk, chunk)
+        to = lax.rem(f + d, freqs)
+        return pltpu.make_async_remote_copy(
+            src_ref=freq_out.at[to, part], dst_ref=freq_in.at[f, part],
+            send_sem=freq_send.at[d - 1, c], recv_sem=freq_recv.at[d - 1, c],
+            device_id={"freq": to}, device_id_type=MESH,
+        )
+
+    for s in range(4):
+        for copy in table_copies(s):
+            copy.start()
+    barrier = pltpu.get_barrier_semaphore()
+    pl.semaphore_signal(barrier, inc=1, device_id={"pair": 1 - p}, device_id_type=MESH)
+    pl.semaphore_signal(barrier, inc=1, device_id={"read": 1 - r}, device_id_type=MESH)
+    for d in range(1, freqs):
+        pl.semaphore_signal(
+            barrier, inc=1, device_id={"freq": lax.rem(f + d, freqs)}, device_id_type=MESH
+        )
+    clean_rows(info, low, block, high, ext, ch, cl, height)
+    pl.semaphore_wait(barrier, freqs + 1)
+
+    def step(s, carry):
+        for copy in table_copies(s):
+            copy.wait()
+        t = tile_at(s)
+        for parity in range(2):
+            grid[parity] = (
+                dot(ch[parity], bufh[s, parity])
+                + dot(ch[parity], bufl[s, parity])
+                + dot(cl[parity], bufh[s, parity])
+            )
+
+        def fir(i, inner):
+            at = pl.multiple_of(i * 32, 32)
+            for parity in range(2):
+                re = grid[parity, pl.ds(at, 48), :TILE]
+                im = grid[parity, pl.ds(at, 48), TILE:]
+                sum_re = jnp.zeros((32, TILE), F32)
+                sum_im = jnp.zeros((32, TILE), F32)
+                for k in range(8):
+                    shift_re = re[k : k + 40]
+                    shift_im = im[k : k + 40]
+                    for a in (k, k + 8):
+                        qr = taps[t, parity, 0, a : a + 1, :]
+                        qi = taps[t, parity, 1, a : a + 1, :]
+                        xr = shift_re[a - k : a - k + 32]
+                        xi = shift_im[a - k : a - k + 32]
+                        sum_re = sum_re + (qr * xr + qi * xi)
+                        sum_im = sum_im + (qr * xi - qi * xr)
+                lane = parity * 2 * TILE
+                work[s, pl.ds(at, 32), lane : lane + TILE] = sum_re
+                work[s, pl.ds(at, 32), lane + TILE : lane + 2 * TILE] = sum_im
+            return inner
+
+        lax.fori_loop(0, rows // 32, fir, 0)
+
+        @pl.when(s == 0)
+        def _():
+            pair_copy(0).start()
+
+        @pl.when(s == 1)
+        def _():
+            pair_copy(0).wait_recv()
+            for c in range(CHUNKS):
+                part = pl.ds(c * chunk, chunk)
+                work[1, part, :] = work[1, part, :] + pair_in[0, part, :]
+                read_copy(c).start()
+
+        @pl.when(s == 2)
+        def _():
+            pair_copy(1).start()
+
+        return carry
+
+    lax.fori_loop(0, 4, step, 0)
+
+    pair_copy(1).wait_recv()
+    lanes = lax.broadcasted_iota(jnp.int32, (32, TILE), 1) // share
+    for c in range(CHUNKS):
+        read_copy(c).wait_recv()
+
+        def pack(i, carry, c=c):
+            part = pl.ds(pl.multiple_of(c * chunk + i * 32, 32), 32)
+            total = work[3, part, :] + pair_in[1, part, :] + read_in[part, :]
+            quads = [
+                total[:, q * TILE : (q + 1) * TILE]
+                for q in (0, 2, 1, 3)
+            ]
+            for to in range(freqs):
+                result = None
+                for q in range(4):
+                    shift = (q - to) * share % TILE
+                    moved = quads[q] if shift == 0 else pltpu.roll(quads[q], shift, 1)
+                    result = moved if q == 0 else jnp.where(lanes == q, moved, result)
+                freq_out[to, part, :] = result
+            return carry
+
+        lax.fori_loop(0, chunk // 32, pack, 0)
+        for d in range(1, freqs):
+            freq_copy(d, c).start()
+    out[f] = freq_out[f]
+    for n in range(2):
+        pair_copy(n).wait_send()
+    for c in range(CHUNKS):
+        read_copy(c).wait_send()
+    for d in range(1, freqs):
+        for c in range(CHUNKS):
+            freq_copy(d, c).wait()
+        source = lax.rem(f + freqs - d, freqs)
+        out[source] = freq_in[source]
+
+
+def fused(info, low, block, high, taps, tables, freqs):
+    rows, width = block.shape
+    half = width // 2
+    vmem = pl.BlockSpec(memory_space=pltpu.VMEM)
+    anywhere = pl.BlockSpec(memory_space=pl.ANY)
+    dma = pltpu.SemaphoreType.DMA
+    return pl.pallas_call(
+        functools.partial(fused_kernel, freqs),
+        out_shape=jax.ShapeDtypeStruct((freqs, rows, TILE), F32),
+        in_specs=[pl.BlockSpec(memory_space=pltpu.SMEM), vmem, vmem, vmem, vmem, anywhere, anywhere],
+        out_specs=vmem,
+        scratch_shapes=[
+            pltpu.VMEM((rows + 2 * HALO, width), F32),
+            pltpu.VMEM((2, rows + 16, half), BF16),
+            pltpu.VMEM((2, rows + 16, half), BF16),
+            pltpu.VMEM((2, rows + 16, 2 * TILE), F32),
+            pltpu.VMEM((4, 2, half, 2 * TILE), BF16),
+            pltpu.VMEM((4, 2, half, 2 * TILE), BF16),
+            pltpu.VMEM((4, rows, 4 * TILE), F32),
+            pltpu.VMEM((2, rows, 4 * TILE), F32),
+            pltpu.VMEM((rows, 4 * TILE), F32),
+            pltpu.VMEM((freqs, rows, TILE), F32),
+            pltpu.VMEM((freqs, rows, TILE), F32),
+            dma((2, 4)),
+            dma((2,)),
+            dma((2,)),
+            dma((CHUNKS,)),
+            dma((CHUNKS,)),
+            dma((freqs - 1, CHUNKS)),
+            dma((freqs - 1, CHUNKS)),
+        ],
+        compiler_params=pltpu.CompilerParams(
+            collective_id=0, has_side_effects=True, vmem_limit_bytes=56 * 1024 * 1024
+        ),
+        cost_estimate=pl.CostEstimate(flops=7 * 10**9, bytes_accessed=14 * 2**20, transcendentals=0),
+        name="fused",
+    )(info, low, block, high, taps, *tables)
+
+
 def column_tables(height):
     quarter = height // 4
     inner = np.arange(quarter)
@@ -281,14 +511,18 @@
     taps = taps.reshape(2, stamp_len, 2, tiles, TILE).transpose(3, 2, 0, 1, 4)
     info = jnp.stack([freq_at * rows_dev, low_row, high_row, jnp.int32(height)]).astype(jnp.int32)
 
-    terms = front(info, low, block, high, taps, row_tables(ids, width))
-    if tiles != readers:
-        terms = terms.reshape(tiles, rows_dev, 2, 2, readers // tiles, TILE * tiles // readers)
-        terms = terms.transpose(0, 4, 1, 2, 3, 5).reshape(readers, rows_dev, -1)
-    summed = lax.psum_scatter(terms, READERS, scatter_dimension=0, tiled=True)
-    summed = summed.reshape(rows_dev, 2, 2, freqs, share // 2)
-    summed = summed.transpose(3, 0, 2, 1, 4).reshape(freqs, rows_dev, 2 * share)
-    gathered = lax.all_to_all(summed, "freq", split_axis=0, concat_axis=0, tiled=True)
+    tables = row_tables(ids, width)
+    if lax.axis_size("read") == 2 and lax.axis_size("pair") == 2 and tiles == 4 and freqs == 4:
+        gathered = fused(info, low, block, high, taps, tables, freqs)
+    else:
+        terms = front(info, low, block, high, taps, tables)
+        if tiles != readers:
+            terms = terms.reshape(tiles, rows_dev, 2, 2, readers // tiles, TILE * tiles // readers)
+            terms = terms.transpose(0, 4, 1, 2, 3, 5).reshape(readers, rows_dev, -1)
+        summed = lax.psum_scatter(terms, READERS, scatter_dimension=0, tiled=True)
+        summed = summed.reshape(rows_dev, 2, 2, freqs, share // 2)
+        summed = summed.transpose(3, 0, 2, 1, 4).reshape(freqs, rows_dev, 2 * share)
+        gathered = lax.all_to_all(summed, "freq", split_axis=0, concat_axis=0, tiled=True)
     grid = columns(gathered.reshape(height, 2 * share), order_matrix(share), column_tables(height))
     grid = lax.all_to_all(
         grid.reshape(readers, out_rows, 2 * share), READERS, split_axis=0, concat_axis=0, tiled=True

time: 170 us -> 106 us (0.62)
  waiting for transfers between devices: 79.8 us -> 10.8 us
  Pallas kernels: 42 us -> 66.3 us
  between operations: 14.3 us -> 0.82 us
  starting transfers between devices: 13.3 us -> 8.68 us
  local copies, waits for them, and re-layouts: 9.81 us -> 7.49 us
    reduce_scatter x1 -> x0, waiting for transfers between devices: 44.3 us -> none  [per_device(): summed = lax.psum_scatter(terms, READERS, scatter_dimension=0, tiled=True)]
    all_to_all x1 -> x0, waiting for transfers between devices: 24.8 us -> none  [per_device(): lax.all_to_all(summed, 'freq', split_axis=0, concat_axis=0, tiled=True)]
    pallas_call x1, Pallas kernels: 31.5 us -> 55.9 us  [fused(): pl.pallas_call(functools.partial(fused_kernel, freqs), out_shape=jax.Shap...]
    all_to_all x1 -> x0, starting transfers between devices: 4.6 us -> none  [per_device(): lax.all_to_all(summed, 'freq', split_axis=0, concat_axis=0, tiled=True)]
  transfers between devices with their start and end apart: 5 -> 3, of which waited for: 3 -> 1; matrix products, arithmetic and copies ran while one was open for 7% -> 12% of each run, Pallas kernels for 1% -> 2%
where the time goes in v2:
time: 106 us; the launch traced here: 105 us
  Pallas kernels  66.3 us (63%)
  waiting for transfers between devices  10.8 us (10%)
  other arithmetic  8.97 us (8%)
  starting transfers between devices  8.68 us (8%)
  local copies, waits for them, and re-layouts  7.49 us (7%)
  matrix products  2.16 us (2%)
    pallas_call x1, Pallas kernels, fused(): pl.pallas_call(functools.partial(fused_kernel, freqs), out_shape=jax.Shap...  55.9 us
    all_to_all x1, waiting for transfers between devices, per_device(): lax.all_to_all(grid.reshape(readers, out_rows, 2 * share), READERS, split...  10.8 us
    pallas_call x1, Pallas kernels, columns(): pl.pallas_call(column_kernel, grid=(4,), out_shape=jax.ShapeDtypeStruct((...  8.18 us
    all_to_all x1, starting transfers between devices, per_device(): lax.all_to_all(grid.reshape(readers, out_rows, 2 * share), READERS, split...  3.52 us
    ppermute x1, starting transfers between devices, per_device(): low = lax.ppermute(block[rows_dev - HALO:], 'freq', forward)  3.08 us
    pallas_call x1, Pallas kernels, per_device(): pl.pallas_call(denom_kernel, out_shape=jax.ShapeDtypeStruct((out_rows, pe...  2.31 us
  transfers between devices with their start and end apart: 3, of which 1 were waited for; matrix products, arithmetic and copies ran while one was open for 12% of the time, Pallas kernels for 2%

profile of v2, /device:TPU:0, one launch (start us, length us, event | category | flops | bytes accessed | tf_op | source)
XLA Modules:
  0.0 105.3 jit_solution(1182715575013850175)
XLA Ops:
  0.0 1.0 slice_bitcast_fusion
  1.0 3.1 %collective-permute-start = (f32[16,2048]{1,0:T(8,128)S(1)}, f32[16,2048]{1,0:T(8,128)S(1)}, u32[]{:S(2)}, u32[]{:S(2)}) collective-permute-start(f32[16,2048]{1,0:T(8,128)S(1)} %get-tuple-element.8), channel_id=1, source_target_pairs={{0,4},{4,8},{8,12},{12,0},{1,5},{5,9},{9,13},{13,1},{2,6},{6,10},{... | collective-permute-start | bytes 393224 | tf_op jit(solution)/shard_map/ppermute | solution.py:494
  4.1 2.1 %collective-permute-start.1 = (f32[16,2048]{1,0:T(8,128)S(1)}, f32[16,2048]{1,0:T(8,128)S(1)}, u32[]{:S(2)}, u32[]{:S(2)}) collective-permute-start(f32[16,2048]{1,0:T(8,128)S(1)} %get-tuple-element.7), channel_id=1, source_target_pairs={{4,0},{8,4},{12,8},{0,12},{5,1},{9,5},{13,9},{1,13},{6,2},{10,6},{... | collective-permute-start | bytes 393224 | tf_op jit(solution)/shard_map/ppermute | solution.py:495
  6.2 1.3 %fusion.6 = s32[]{:T(128)} fusion(s32[4]{0:T(128)} %param.21, s32[]{:T(128)S(6)} %add.9), kind=kLoop, calls=%fused_computation.17 | loop fusion | flops 11 | bytes 24 | tf_op jit(solution)/shard_map/reduce_sum | solution.py:498
  7.5 0.6 iota_compare_fusion
  8.1 2.1 %fusion.8 = (s32[]{:T(128)}, s32[]{:T(128)}) fusion(s32[4,2]{0,1:T(2,128)} %param.19, s32[]{:T(128)} %fusion.6), kind=kLoop, calls=%fused_computation.22 | loop fusion | flops 18 | bytes 44 | tf_op jit(solution)/shard_map/reduce_sum | solution.py:500
  10.2 0.8 select_reduce_fusion
  11.1 2.0 %multiply_divide_fusion = (f32[4]{0:T(128)S(1)}, f32[]{:T(128)}) fusion(f32[4]{0:T(128)} %param.18, f32[4]{0:T(128)} %param.17, s32[4]{0:T(128)} %param.20, s32[]{:T(128)} %fusion.6), kind=kLoop, calls=%fused_computation.23 | loop fusion | flops 31 | bytes 72 | tf_op jit(solution)/shard_map/div | solution.py:504
  13.7 1.2 %convolution_bitcast_fusion = f32[2,16,1024]{2,1,0:T(8,128)S(1)} fusion(f32[2,16,1024]{2,1,0:T(8,128)} %constant.45.clone, f32[16,16]{1,0:T(8,128)S(1)} %select_reduce_fusion, f32[]{:T(128)S(6)} %mul.39), kind=kOutput, calls=%fused_computation | convolution fusion | flops 6291712 | bytes 263172 | tf_op jit(solution)/shard_map/ab,cbp->cap/dot_general | solution.py:510
  14.9 1.9 %pad_add_fusion.info = s32[4]{0:T(128)} fusion(s32[1]{0:T(128)} %constant.19.clone.1, s32[1]{0:T(128)} %bitcast.4, s32[1]{0:T(128)} %bitcast.2, s32[1]{0:T(128)} %bitcast), kind=kLoop, calls=%fused_computation.18 | loop fusion | flops 12 | bytes 32 | tf_op jit(solution)/shard_map/stack | solution.py:512
  16.7 0.1 reshape.22
  16.8 0.7 copy.24
  17.5 1.0 constant_dynamic-slice_fusion.rows
  18.5 0.0 collective-permute-done.low
  18.5 0.0 copy-start.3
  18.5 0.0 collective-permute-done.1.high
  18.5 0.0 copy-start.4
  18.5 0.6 copy-done.3
  19.1 0.0 copy-done.4
  19.2 0.0 copy-start.1
  19.2 55.9 %fused.1 = f32[4,512,128]{2,1,0:T(8,128)} custom-call(s32[4]{0:T(128)} %pad_add_fusion.info, f32[16,2048]{1,0:T(8,128)} %copy-done.3, f32[512,2048]{1,0:T(8,128)} %bitcast.52, f32[16,2048]{1,0:T(8,128)} %copy-done.4, f32[4,2,2,16,128]{4,3,2,1,0:T(8,128)} %bitcast.51, bf16[4,2,1024,256]{3,2,1,0:T(8,128)(2,1)} %constant.46.clone.th, ...), custom_call_target="tpu_custom_call" | custom-call | flops 7000000000 | bytes 14680064 | tf_op jit(solution)/shard_map/fused/pallas_call | solution.py:359
  75.0 0.0 copy-done.1
  75.0 0.0 copy-start
  75.0 1.2 %copy-done = f32[4,512,128]{2,1,0:T(8,128)S(1)} copy-done((f32[4,512,128]{2,1,0:T(8,128)S(1)}, f32[4,512,128]{2,1,0:T(8,128)}, u32[]{:S(2)}) %copy-start) | copy-done | bytes 1048600
  76.3 8.2 %columns.1 = f32[2048,128]{1,0:T(8,128)S(1)} custom-call(f32[2048,128]{1,0:T(8,128)S(1)} %bitcast.49, bf16[128,256]{1,0:T(8,128)(2,1)S(1)} %copy-done.1, bf16[4,512,1024]{2,1,0:T(8,128)(2,1)} %constant.49.clone.th, bf16[4,512,1024]{2,1,0:T(8,128)(2,1)} %constant.50.clone.tl), custom_call_target="tpu_custom_call" | custom-call | tf_op jit(solution)/shard_map/columns/pallas_call | solution.py:447
  84.4 0.0 copy-start.2
  84.4 1.3 %copy.18 = f32[4,512,128]{1,2,0:T(8,128)} copy(f32[4,512,128]{2,1,0:T(8,128)S(1)} %bitcast.48) | data formatting | bytes 2097152 | tf_op jit(solution)/shard_map/reshape | solution.py:528
  85.8 3.5 %all-to-all-start = ((f32[4,512,128]{1,2,0:T(8,128)}), f32[4,512,128]{1,2,0:T(8,128)S(1)}, u32[]{:S(2)}, u32[]{:S(2)}) async-start(f32[4,512,128]{1,2,0:T(8,128)} %copy.18), calls=%async_computation | async-start | bytes 2097152 | tf_op jit(solution)/shard_map/all_to_all | solution.py:527
  89.3 0.0 copy-done.2
  89.3 1.0 convolution_bitcast_fusion.1
  90.4 2.3 %denom.1 = f32[512,256]{1,0:T(8,128)S(1)} custom-call(f32[4]{0:T(128)S(1)} %get-tuple-element.11.weight, f32[512,32]{1,0:T(8,128)S(1)} %constant_dynamic-slice_fusion.rows, f32[4,32,512]{2,1,0:T(8,128)S(1)} %maximum_maximum_fusion.cols), custom_call_target="tpu_custom_call" | custom-call | tf_op jit(solution)/shard_map/denom/pallas_call | solution.py:543
  92.7 0.2 copy.20
  92.9 10.8 %all-to-all-done = f32[4,512,128]{1,2,0:T(8,128)S(1)} async-done(((f32[4,512,128]{1,2,0:T(8,128)}), f32[4,512,128]{1,2,0:T(8,128)S(1)}, u32[]{:S(2)}, u32[]{:S(2)}) %all-to-all-start) | async-done | bytes 1048608 | tf_op jit(solution)/shard_map/all_to_all | solution.py:527
  103.7 0.1 copy.19
  103.8 0.2 bitcast_multiply_fusion
  104.0 1.3 %copy.21 = f32[2,512,256]{2,1,0:T(8,128)} copy(f32[2,512,256]{1,2,0:T(8,128)S(1)} %bitcast_multiply_fusion) | data formatting | bytes 2097152 | tf_op jit(solution)/shard_map/mul | solution.py:555
  (3 shorter events, 0.0 us)
Async XLA Ops:
  1.0 17.5 %collective-permute-start = (f32[16,2048]{1,0:T(8,128)S(1)}, f32[16,2048]{1,0:T(8,128)S(1)}, u32[]{:S(2)}, u32[]{:S(2)}) collective-permute-start(f32[16,2048]{1,0:T(8,128)S(1)} %get-tuple-element.8), channel_id=1, source_target_pairs={{0,4},{4,8},{8,12},{12,0},{1,5},{5,9},{9,13},{13,1},{2,6},{6,10},{... | collective-permute-start | bytes 393224 | tf_op jit(solution)/shard_map/ppermute | solution.py:494
  4.1 14.4 %collective-permute-start.1 = (f32[16,2048]{1,0:T(8,128)S(1)}, f32[16,2048]{1,0:T(8,128)S(1)}, u32[]{:S(2)}, u32[]{:S(2)}) collective-permute-start(f32[16,2048]{1,0:T(8,128)S(1)} %get-tuple-element.7), channel_id=1, source_target_pairs={{4,0},{8,4},{12,8},{0,12},{5,1},{9,5},{13,9},{1,13},{6,2},{10,6},{... | collective-permute-start | bytes 393224 | tf_op jit(solution)/shard_map/ppermute | solution.py:495
  18.5 0.7 copy-start.3
  18.5 0.7 copy-start.4
  19.2 55.9 %copy-start.1 = (bf16[128,256]{1,0:T(8,128)(2,1)S(1)}, bf16[128,256]{1,0:T(8,128)(2,1)}, u32[]{:S(2)}) copy-start(bf16[128,256]{1,0:T(8,128)(2,1)} %constant.48.clone.order) | copy-start | bytes 196612
  75.0 1.2 %copy-start = (f32[4,512,128]{2,1,0:T(8,128)S(1)}, f32[4,512,128]{2,1,0:T(8,128)}, u32[]{:S(2)}) copy-start(f32[4,512,128]{2,1,0:T(8,128)} %fused.1) | copy-start | bytes 3145732
  84.4 4.8 %copy-start.2 = (f32[4,16,16]{2,1,0:T(8,128)S(1)}, f32[4,16,16]{2,1,0:T(8,128)}, u32[]{:S(2)}) copy-start(f32[4,16,16]{2,1,0:T(8,128)} %param.16) | copy-start | bytes 12292
  85.8 18.0 %all-to-all-start = ((f32[4,512,128]{1,2,0:T(8,128)}), f32[4,512,128]{1,2,0:T(8,128)S(1)}, u32[]{:S(2)}, u32[]{:S(2)}) async-start(f32[4,512,128]{1,2,0:T(8,128)} %copy.18), calls=%async_computation | async-start | bytes 2097152 | tf_op jit(solution)/shard_map/all_to_all | solution.py:527

commit v3 on v2

--- a/solution.py
+++ b/solution.py
@@ -163,26 +163,138 @@
 MESH = pl.DeviceIdType.MESH
 
 
-def clean_rows(info, low, block, high, ext, ch, cl, height):
+def fused_kernel(
+    freqs, assign, footprint, accept, zero_point, noise_var,
+    stamps, tap_table, psf_rows, psf_cols, order, block, th, tl, uh, ul, out,
+    ext, ch, cl, grid, bufh, bufl, work, pair_in, read_in, freq_out, freq_in,
+    taps, colh, coll, mixed, col_out, last_in, inverse,
+    block_sem, table_sem, col_sem, halo_send, halo_recv, pair_send, pair_recv,
+    read_send, read_recv, freq_send, freq_recv, last_send, last_recv,
+):
     rows, width = block.shape
     half = width // 2
-    ext[:HALO] = low[...]
-    ext[HALO : HALO + rows] = block[...]
-    ext[HALO + rows :] = high[...]
+    height = rows * freqs
+    chunk = rows // CHUNKS
+    share = TILE // freqs
+    count, stamp_len, _ = stamps.shape
+    r = lax.axis_index("read")
+    p = lax.axis_index("pair")
+    f = lax.axis_index("freq")
+    reader = r * 2 + p
+
+    def tile_at(s):
+        rd = jnp.where(s < 2, 1 - r, r)
+        pd = jnp.where(s % 2 == 0, 1 - p, p)
+        return rd * 2 + pd
+
+    def table_copies(s):
+        t = tile_at(s)
+        return (
+            pltpu.make_async_copy(th.at[t], bufh.at[s], table_sem.at[0, s]),
+            pltpu.make_async_copy(tl.at[t], bufl.at[s], table_sem.at[1, s]),
+        )
+
+    col_copies = (
+        pltpu.make_async_copy(uh, colh, col_sem.at[0]),
+        pltpu.make_async_copy(ul, coll, col_sem.at[1]),
+    )
+    block_copy = pltpu.make_async_copy(block, ext.at[pl.ds(HALO, rows)], block_sem)
+
+    def halo_copy(n):
+        source = rows - HALO if n == 0 else 0
+        place = 0 if n == 0 else HALO + rows
+        to = lax.rem(f + (1 if n == 0 else freqs - 1), freqs)
+        return pltpu.make_async_remote_copy(
+            src_ref=block.at[pl.ds(source, HALO)], dst_ref=ext.at[pl.ds(place, HALO)],
+            send_sem=halo_send.at[n], recv_sem=halo_recv.at[n],
+            device_id={"freq": to}, device_id_type=MESH,
+        )
+
+    def pair_copy(n):
+        return pltpu.make_async_remote_copy(
+            src_ref=work.at[2 * n], dst_ref=pair_in.at[n],
+            send_sem=pair_send.at[n], recv_sem=pair_recv.at[n],
+            device_id={"pair": 1 - p}, device_id_type=MESH,
+        )
+
+    def read_copy(c):
+        part = pl.ds(c * chunk, chunk)
+        return pltpu.make_async_remote_copy(
+            src_ref=work.at[1, part], dst_ref=read_in.at[part],
+            send_sem=read_send.at[c], recv_sem=read_recv.at[c],
+            device_id={"read": 1 - r}, device_id_type=MESH,
+        )
+
+    def freq_copy(d, c):
+        part = pl.ds(c * chunk, chunk)
+        to = lax.rem(f + d, freqs)
+        return pltpu.make_async_remote_copy(
+            src_ref=freq_out.at[to, part], dst_ref=freq_in.at[f, part],
+            send_sem=freq_send.at[d - 1, c], recv_sem=freq_recv.at[d - 1, c],
+            device_id={"freq": to}, device_id_type=MESH,
+        )
+
+    def last_copy(e, j):
+        rd = r if e == 0 else 1 - r
+        pd = p if e == 1 else 1 - p
+        return pltpu.make_async_remote_copy(
+            src_ref=col_out.at[j, pl.ds(pl.multiple_of((rd * 2 + pd) * TILE, TILE), TILE)],
+            dst_ref=last_in.at[reader, j],
+            send_sem=last_send.at[e, j], recv_sem=last_recv.at[e, j],
+            device_id={"read": rd, "pair": pd}, device_id_type=MESH,
+        )
+
+    barrier = pltpu.get_barrier_semaphore()
+    for to in (
+        {"pair": 1 - p},
+        {"read": 1 - r},
+        {"read": 1 - r, "pair": 1 - p},
+        *({"freq": lax.rem(f + d, freqs)} for d in range(1, freqs)),
+    ):
+        pl.semaphore_signal(barrier, inc=1, device_id=to, device_id_type=MESH)
+    block_copy.start()
+    for s in range(4):
+        for copy in table_copies(s):
+            copy.start()
+    for copy in col_copies:
+        copy.start()
+    pl.semaphore_wait(barrier, freqs + 2)
+    for n in range(2):
+        halo_copy(n).start()
+
+    owner = assign[reader]
+    low_row = footprint[owner, 0]
+    high_row = footprint[owner, 1]
+
+    def spread(value):
+        return jnp.full((1, 2 * TILE), value, F32)
+
+    def gate(e):
+        return spread(accept[e].astype(F32)) * spread(zero_point[e])
+
+    weight = gate(owner) / spread(noise_var[owner]) * (1.0 / math.sqrt(height * width))
+    all_taps = jnp.dot(stamps[owner], tap_table[...], precision=HIGHEST, preferred_element_type=F32)
+    for part in range(2):
+        for parity in range(2):
+            for t in range(4):
+                at = ((part * 2 + parity) * 4 + t) * TILE
+                taps[t, parity, part] = all_taps[:, at : at + TILE] * weight[:, :TILE]
+
+    block_copy.wait()
     cols = lax.broadcasted_iota(jnp.int32, (16, width), 1)
 
     def clean(i, carry):
         at = pl.multiple_of(i * 16, 16)
         piece = ext[pl.ds(at, 32), :]
         mid = piece[8:24]
-        ids = info[0] - 8 + at + lax.broadcasted_iota(jnp.int32, (16, 1), 0)
+        ids = f * rows - 8 + at + lax.broadcasted_iota(jnp.int32, (16, 1), 0)
         ids = jnp.where(ids < 0, ids + height, ids)
         ids = jnp.where(ids >= height, ids - height, ids)
         up = jnp.where(ids == 0, 0.0, piece[7:23])
         down = jnp.where(ids == height - 1, 0.0, piece[9:25])
         left = jnp.where(cols == 0, 0.0, pltpu.roll(mid, 1, 1))
         right = jnp.where(cols == width - 1, 0.0, pltpu.roll(mid, width - 1, 1))
-        inside = (ids >= info[1]) & (ids < info[2])
+        inside = (ids >= low_row) & (ids < high_row)
         cell = jnp.where(inside, mid - 0.25 * (up + down + left + right), 0.0)
         for parity in range(2):
             if parity == 0:
@@ -194,70 +306,10 @@
             cl[parity, pl.ds(at, 16), :] = lo
         return carry
 
-    lax.fori_loop(0, (rows + 16) // 16, clean, 0)
-
-
-def fused_kernel(
-    freqs, info, low, block, high, taps, th, tl, out,
-    ext, ch, cl, grid, bufh, bufl, work, pair_in, read_in, freq_out, freq_in,
-    table_sem, pair_send, pair_recv, read_send, read_recv, freq_send, freq_recv,
-):
-    rows, width = block.shape
-    height = rows * freqs
-    chunk = rows // CHUNKS
-    share = TILE // freqs
-    r = lax.axis_index("read")
-    p = lax.axis_index("pair")
-    f = lax.axis_index("freq")
-
-    def tile_at(s):
-        rd = jnp.where(s < 2, 1 - r, r)
-        pd = jnp.where(s % 2 == 0, 1 - p, p)
-        return rd * 2 + pd
-
-    def table_copies(s):
-        t = tile_at(s)
-        return (
-            pltpu.make_async_copy(th.at[t], bufh.at[s], table_sem.at[0, s]),
-            pltpu.make_async_copy(tl.at[t], bufl.at[s], table_sem.at[1, s]),
-        )
-
-    def pair_copy(n):
-        return pltpu.make_async_remote_copy(
-            src_ref=work.at[2 * n], dst_ref=pair_in.at[n],
-            send_sem=pair_send.at[n], recv_sem=pair_recv.at[n],
-            device_id={"pair": 1 - p}, device_id_type=MESH,
-        )
-
-    def read_copy(c):
-        part = pl.ds(c * chunk, chunk)
-        return pltpu.make_async_remote_copy(
-            src_ref=work.at[1, part], dst_ref=read_in.at[part],
-            send_sem=read_send.at[c], recv_sem=read_recv.at[c],
-            device_id={"read": 1 - r}, device_id_type=MESH,
-        )
-
-    def freq_copy(d, c):
-        part = pl.ds(c * chunk, chunk)
-        to = lax.rem(f + d, freqs)
-        return pltpu.make_async_remote_copy(
-            src_ref=freq_out.at[to, part], dst_ref=freq_in.at[f, part],
-            send_sem=freq_send.at[d - 1, c], recv_sem=freq_recv.at[d - 1, c],
-            device_id={"freq": to}, device_id_type=MESH,
-        )
-
-    for s in range(4):
-        for copy in table_copies(s):
-            copy.start()
-    barrier = pltpu.get_barrier_semaphore()
-    pl.semaphore_signal(barrier, inc=1, device_id={"pair": 1 - p}, device_id_type=MESH)
-    pl.semaphore_signal(barrier, inc=1, device_id={"read": 1 - r}, device_id_type=MESH)
-    for d in range(1, freqs):
-        pl.semaphore_signal(
-            barrier, inc=1, device_id={"freq": lax.rem(f + d, freqs)}, device_id_type=MESH
-        )
-    clean_rows(info, low, block, high, ext, ch, cl, height)
-    pl.semaphore_wait(barrier, freqs + 1)
+    lax.fori_loop(1, rows // 16, clean, 0)
+    for n in range(2):
+        halo_copy(n).wait()
+    lax.fori_loop(0, 2, lambda n, carry: clean(n * (rows // 16), carry), 0)
 
     def step(s, carry):
         for copy in table_copies(s):
@@ -322,10 +374,7 @@
         def pack(i, carry, c=c):
             part = pl.ds(pl.multiple_of(c * chunk + i * 32, 32), 32)
             total = work[3, part, :] + pair_in[1, part, :] + read_in[part, :]
-            quads = [
-                total[:, q * TILE : (q + 1) * TILE]
-                for q in (0, 2, 1, 3)
-            ]
+            quads = [total[:, q * TILE : (q + 1) * TILE] for q in (0, 2, 1, 3)]
             for to in range(freqs):
                 result = None
                 for q in range(4):
@@ -338,28 +387,107 @@
         lax.fori_loop(0, chunk // 32, pack, 0)
         for d in range(1, freqs):
             freq_copy(d, c).start()
-    out[f] = freq_out[f]
+    freq_in[f] = freq_out[f]
+
+    wide = 2 * TILE
+    q = jnp.dot(
+        stamps[...].reshape(count * stamp_len, stamp_len), psf_cols[f],
+        precision=HIGHEST, preferred_element_type=F32,
+    )
+    rh, rl = split(psf_rows[reader])
+    total = jnp.zeros((rows, wide), F32)
+    for e in range(count):
+        q_re = q[e * stamp_len : (e + 1) * stamp_len, :wide]
+        q_im = q[e * stamp_len : (e + 1) * stamp_len, wide:]
+        both = jnp.concatenate(
+            [jnp.concatenate([q_re, q_im], axis=1), jnp.concatenate([q_im, -q_re], axis=1)], axis=0
+        )
+        qh, ql = split(both)
+        psf = dot(rh, qh) + dot(rh, ql) + dot(rl, qh)
+        gain = gate(e) * spread(zero_point[e]) / spread(noise_var[e])
+        total = total + gain * (psf[:, :wide] * psf[:, :wide] + psf[:, wide:] * psf[:, wide:])
+    total = lax.rsqrt(total)
+    for side in range(2):
+        inverse[side] = total[:, side * TILE : (side + 1) * TILE]
+
+    for c in range(CHUNKS):
+        for d in range(1, freqs):
+            freq_copy(d, c).wait_recv()
+        parts = []
+        for g in range(4):
+            hi, lo = split(freq_in[g, pl.ds(c * chunk, chunk), :])
+            parts.append(dot(hi, order[...]) + dot(lo, order[...]))
+        for j in range(4):
+            if j % 2 == 0:
+                even, odd = parts[0] + parts[2], parts[1] + parts[3]
+                mix = even + odd if j == 0 else even - odd
+                top, low = mix[:, :TILE], mix[:, TILE:]
+            else:
+                even, odd = parts[0] - parts[2], parts[1] - parts[3]
+                sign = 1.0 if j == 1 else -1.0
+                top = even[:, :TILE] + sign * odd[:, TILE:]
+                low = even[:, TILE:] - sign * odd[:, :TILE]
+            for n, value in enumerate((top, low)):
+                hi, lo = split(value)
+                part = pl.ds(n * rows + c * chunk, chunk)
+                mixed[j, part, :TILE] = hi
+                mixed[j, part, TILE:] = lo
+    for copy in col_copies:
+        copy.wait()
+
+    for j in range(4):
+        both = dot(colh[j], mixed[j])
+        col_out[j] = both[:, :TILE] + both[:, TILE:] + dot(coll[j], mixed[j, :, :TILE])
+        for e in (1, 2, 0):
+            last_copy(e, j).start()
+    lanes = lax.broadcasted_iota(jnp.int32, (TILE, TILE), 1)
+    for j in range(4):
+        last_in[reader, j] = col_out[j, pl.ds(pl.multiple_of(reader * TILE, TILE), TILE), :]
+        for e in range(3):
+            last_copy(e, j).wait_recv()
+        for side in range(2):
+            one, two = last_in[2 * side, j], last_in[2 * side + 1, j]
+            re = jnp.where(lanes < TILE // 2, one, pltpu.roll(two, TILE // 2, 1))
+            im = jnp.where(lanes < TILE // 2, pltpu.roll(one, TILE // 2, 1), two)
+            place = pl.ds(j, TILE, stride=4)
+            gain = inverse[side, place, :]
+            out[0, side, place, :] = re * gain
+            out[1, side, place, :] = im * gain
+
     for n in range(2):
         pair_copy(n).wait_send()
     for c in range(CHUNKS):
         read_copy(c).wait_send()
-    for d in range(1, freqs):
-        for c in range(CHUNKS):
-            freq_copy(d, c).wait()
-        source = lax.rem(f + freqs - d, freqs)
-        out[source] = freq_in[source]
-
-
-def fused(info, low, block, high, taps, tables, freqs):
+        for d in range(1, freqs):
+            freq_copy(d, c).wait_send()
+    for e in range(3):
+        for j in range(4):
+            last_copy(e, j).wait_send()
+
+
+def fused(scalars, stamps, ids, block, freqs, readers):
     rows, width = block.shape
     half = width // 2
+    height = rows * freqs
+    stamp_len = stamps.shape[1]
+    offsets = np.arange(stamp_len) - stamp_len // 2
+    phase = angles(offsets, ids.reshape(-1), width)
+    tap_table = np.concatenate([np.cos(phase), -np.sin(phase)], axis=1).astype(np.float32)
+    phase = angles(np.arange(height), offsets, height)
+    psf_rows = np.concatenate([np.cos(phase), np.sin(phase)], axis=1).astype(np.float32)
+    psf_rows = psf_rows.reshape(readers, height // readers, -1)
+    phase = angles(offsets, np.arange(half), width).reshape(stamp_len, freqs, -1)
+    psf_cols = np.concatenate([np.cos(phase), -np.sin(phase)], axis=2).astype(np.float32)
+    psf_cols = psf_cols.transpose(1, 0, 2)
+    order = order_matrix(TILE // 2)
     vmem = pl.BlockSpec(memory_space=pltpu.VMEM)
+    smem = pl.BlockSpec(memory_space=pltpu.SMEM)
     anywhere = pl.BlockSpec(memory_space=pl.ANY)
     dma = pltpu.SemaphoreType.DMA
-    return pl.pallas_call(
+    result = pl.pallas_call(
         functools.partial(fused_kernel, freqs),
-        out_shape=jax.ShapeDtypeStruct((freqs, rows, TILE), F32),
-        in_specs=[pl.BlockSpec(memory_space=pltpu.SMEM), vmem, vmem, vmem, vmem, anywhere, anywhere],
+        out_shape=jax.ShapeDtypeStruct((2, 2, rows, TILE), F32),
+        in_specs=[smem] * 5 + [vmem] * 5 + [anywhere] * 5,
         out_specs=vmem,
         scratch_shapes=[
             pltpu.VMEM((rows + 2 * HALO, width), F32),
@@ -373,20 +501,36 @@
             pltpu.VMEM((rows, 4 * TILE), F32),
             pltpu.VMEM((freqs, rows, TILE), F32),
             pltpu.VMEM((freqs, rows, TILE), F32),
+            pltpu.VMEM((4, 2, 2, stamp_len, TILE), F32),
+            pltpu.VMEM((4, rows, 2 * rows), BF16),
+            pltpu.VMEM((4, rows, 2 * rows), BF16),
+            pltpu.VMEM((4, 2 * rows, 2 * TILE), BF16),
+            pltpu.VMEM((4, rows, TILE), F32),
+            pltpu.VMEM((4, 4, TILE, TILE), F32),
+            pltpu.VMEM((2, rows, TILE), F32),
+            dma,
             dma((2, 4)),
+            dma((2,)),
+            dma((2,)),
+            dma((2,)),
             dma((2,)),
             dma((2,)),
             dma((CHUNKS,)),
             dma((CHUNKS,)),
             dma((freqs - 1, CHUNKS)),
             dma((freqs - 1, CHUNKS)),
+            dma((3, 4)),
+            dma((3, 4)),
         ],
         compiler_params=pltpu.CompilerParams(
-            collective_id=0, has_side_effects=True, vmem_limit_bytes=56 * 1024 * 1024
+            collective_id=0, has_side_effects=True, vmem_limit_bytes=58 * 1024 * 1024
         ),
-        cost_estimate=pl.CostEstimate(flops=7 * 10**9, bytes_accessed=14 * 2**20, transcendentals=0),
         name="fused",
-    )(info, low, block, high, taps, *tables)
+    )(
+        *scalars, stamps, tap_table, psf_rows, psf_cols, order, block,
+        *row_tables(ids, width), *column_tables(height),
+    )
+    return result.transpose(0, 2, 1, 3).reshape(2, rows, 2 * TILE)
 
 
 def column_tables(height):
@@ -489,6 +633,10 @@
     offsets = np.arange(stamp_len) - stamp_len // 2
 
     block = exposures[0]
+    square = lax.axis_size("read") == 2 and lax.axis_size("pair") == 2
+    if square and tiles == 4 and freqs == 4 and rows_dev == 4 * TILE:
+        scalars = (assign, footprint, accept, zero_point, noise_var)
+        return fused(scalars, stamps, ids, block, freqs, readers)
     forward = [(i, (i + 1) % freqs) for i in range(freqs)]
     backward = [(t, s) for s, t in forward]
     low = lax.ppermute(block[rows_dev - HALO :], "freq", forward)
@@ -512,17 +660,14 @@
     info = jnp.stack([freq_at * rows_dev, low_row, high_row, jnp.int32(height)]).astype(jnp.int32)
 
     tables = row_tables(ids, width)
-    if lax.axis_size("read") == 2 and lax.axis_size("pair") == 2 and tiles == 4 and freqs == 4:
-        gathered = fused(info, low, block, high, taps, tables, freqs)
-    else:
-        terms = front(info, low, block, high, taps, tables)
-        if tiles != readers:
-            terms = terms.reshape(tiles, rows_dev, 2, 2, readers // tiles, TILE * tiles // readers)
-            terms = terms.transpose(0, 4, 1, 2, 3, 5).reshape(readers, rows_dev, -1)
-        summed = lax.psum_scatter(terms, READERS, scatter_dimension=0, tiled=True)
-        summed = summed.reshape(rows_dev, 2, 2, freqs, share // 2)
-        summed = summed.transpose(3, 0, 2, 1, 4).reshape(freqs, rows_dev, 2 * share)
-        gathered = lax.all_to_all(summed, "freq", split_axis=0, concat_axis=0, tiled=True)
+    terms = front(info, low, block, high, taps, tables)
+    if tiles != readers:
+        terms = terms.reshape(tiles, rows_dev, 2, 2, readers // tiles, TILE * tiles // readers)
+        terms = terms.transpose(0, 4, 1, 2, 3, 5).reshape(readers, rows_dev, -1)
+    summed = lax.psum_scatter(terms, READERS, scatter_dimension=0, tiled=True)
+    summed = summed.reshape(rows_dev, 2, 2, freqs, share // 2)
+    summed = summed.transpose(3, 0, 2, 1, 4).reshape(freqs, rows_dev, 2 * share)
+    gathered = lax.all_to_all(summed, "freq", split_axis=0, concat_axis=0, tiled=True)
     grid = columns(gathered.reshape(height, 2 * share), order_matrix(share), column_tables(height))
     grid = lax.all_to_all(
         grid.reshape(readers, out_rows, 2 * share), READERS, split_axis=0, concat_axis=0, tiled=True

time: 106 us -> 81.3 us (0.77)
  waiting for transfers between devices: 10.8 us -> 0 us
  Pallas kernels: 66.3 us -> 76.8 us
  other arithmetic: 8.97 us -> 0 us
  starting transfers between devices: 8.68 us -> 0 us
  local copies, waits for them, and re-layouts: 7.49 us -> 4.2 us
  matrix products: 2.16 us -> 0 us
    pallas_call x1, Pallas kernels: 55.9 us -> 76.8 us  [fused(): pl.pallas_call(functools.partial(fused_kernel, freqs), out_shape=jax.Shap...]
    all_to_all x1 -> x0, waiting for transfers between devices: 10.8 us -> none  [per_device(): lax.all_to_all(grid.reshape(readers, out_rows, 2 * share), READERS, split...]
    pallas_call x2 -> x0, Pallas kernels: 10.5 us -> none  [the longest x1 8.18 us: columns(): pl.pallas_call(column_kernel, grid=(4,), out_shape=jax.ShapeDtypeStruct((...]
    ppermute x2 -> x0, starting transfers between devices: 5.17 us -> none  [the longest x1 3.08 us: per_device(): low = lax.ppermute(block[rows_dev - HALO:], 'freq', forward)]
    reduce_sum x3 -> x0, other arithmetic: 4.25 us -> none  [the longest x1 2.12 us: per_device(): low_row = jnp.sum(jnp.where(chosen, footprint[:, 0], 0))]
    all_to_all x1 -> x0, starting transfers between devices: 3.52 us -> none  [per_device(): lax.all_to_all(grid.reshape(readers, out_rows, 2 * share), READERS, split...]
    dot_general x2 -> x0, matrix products: 2.16 us -> none  [the longest x1 1.15 us: per_device(): taps = jnp.einsum('ab,cbp->cap', stamp, tap_table, precision=HIGHEST)]
    div x1 -> x0, other arithmetic: 2.01 us -> none  [per_device(): denom_weight = accepted * zero_point * zero_point / noise_var]
  transfers between devices with their start and end apart: 3 -> 0, of which waited for: 1 -> 0; matrix products, arithmetic and copies ran while one was open for 12% -> 0% of each run, Pallas kernels for 2% -> 0%
where the time goes in v3:
time: 81.3 us; the launch traced here: 81 us
  Pallas kernels  76.8 us (94%)
  local copies, waits for them, and re-layouts  4.2 us (5%)
    pallas_call x1, Pallas kernels, fused(): pl.pallas_call(functools.partial(fused_kernel, freqs), out_shape=jax.Shap...  76.8 us

profile of v3, /device:TPU:0, one launch (start us, length us, event | category | flops | bytes accessed | tf_op | source)
XLA Modules:
  0.0 81.0 jit_solution(5622697428385143457)
XLA Ops:
  0.0 1.3 %copy.17.footprint = s32[4,2]{1,0:T(4,128)} copy(s32[4,2]{0,1:T(2,128)} %param.19) | data formatting | bytes 64 | tf_op args[4]
  1.3 76.8 %fused.1 = f32[2,2,512,128]{3,2,1,0:T(8,128)} custom-call(s32[4]{0:T(128)} %assign.1, s32[4,2]{1,0:T(4,128)} %copy.17.footprint, s32[4]{0:T(128)} %accept.1, f32[4]{0:T(128)} %zero_point.1, f32[4]{0:T(128)} %noise_var.1, f32[4,16,16]{2,1,0:T(8,128)} %stamps.1, f32[16,2048]{1,0:T(8,128)} %constant.16.clone.tap_table, f32[4,512,32]{2,1,0:T(8,128)} %constant.17.clone.psf_rows, ...), custom_call_target="tpu_custom_call" | custom-call | tf_op jit(solution)/shard_map/fused/pallas_call | solution.py:487
  78.1 1.6 %copy.18 = f32[2,512,2,128]{1,3,2,0:T(8,128)S(1)} copy(f32[2,512,2,128]{3,1,2,0:T(8,128)} %bitcast.4) | data formatting | bytes 2097152 | tf_op jit(solution)/shard_map/transpose | solution.py:533
  79.7 1.3 %copy.19 = f32[2,512,256]{2,1,0:T(8,128)} copy(f32[2,512,256]{1,2,0:T(8,128)S(1)} %bitcast.5) | data formatting | bytes 2097152 | tf_op jit(solution)/shard_map/reshape | solution.py:533

commit v4 on v3

--- a/solution.py
+++ b/solution.py
@@ -167,7 +167,7 @@
     freqs, assign, footprint, accept, zero_point, noise_var,
     stamps, tap_table, psf_rows, psf_cols, order, block, th, tl, uh, ul, out,
     ext, ch, cl, grid, bufh, bufl, work, pair_in, read_in, freq_out, freq_in,
-    taps, colh, coll, mixed, col_out, last_in, inverse,
+    taps, colh, coll, stage, col_out, last_in, inverse,
     block_sem, table_sem, col_sem, halo_send, halo_recv, pair_send, pair_recv,
     read_send, read_recv, freq_send, freq_recv, last_send, last_recv,
 ):
@@ -274,11 +274,14 @@
 
     weight = gate(owner) / spread(noise_var[owner]) * (1.0 / math.sqrt(height * width))
     all_taps = jnp.dot(stamps[owner], tap_table[...], precision=HIGHEST, preferred_element_type=F32)
-    for part in range(2):
-        for parity in range(2):
-            for t in range(4):
-                at = ((part * 2 + parity) * 4 + t) * TILE
-                taps[t, parity, part] = all_taps[:, at : at + TILE] * weight[:, :TILE]
+    for parity in range(2):
+        for t in range(4):
+            at = (parity * 4 + t) * TILE
+            re = all_taps[:, at : at + TILE] * weight[:, :TILE]
+            im = all_taps[:, half + at : half + at + TILE] * weight[:, :TILE]
+            taps[t, parity, 0] = re
+            taps[t, parity, 1] = im - re
+            taps[t, parity, 2] = im + re
 
     block_copy.wait()
     cols = lax.broadcasted_iota(jnp.int32, (16, width), 1)
@@ -327,51 +330,52 @@
             for parity in range(2):
                 re = grid[parity, pl.ds(at, 48), :TILE]
                 im = grid[parity, pl.ds(at, 48), TILE:]
-                sum_re = jnp.zeros((32, TILE), F32)
-                sum_im = jnp.zeros((32, TILE), F32)
+                sums = [jnp.zeros((32, TILE), F32) for _ in range(3)]
                 for k in range(8):
                     shift_re = re[k : k + 40]
                     shift_im = im[k : k + 40]
+                    shifted = (shift_re + shift_im, shift_im, shift_re)
                     for a in (k, k + 8):
-                        qr = taps[t, parity, 0, a : a + 1, :]
-                        qi = taps[t, parity, 1, a : a + 1, :]
-                        xr = shift_re[a - k : a - k + 32]
-                        xi = shift_im[a - k : a - k + 32]
-                        sum_re = sum_re + (qr * xr + qi * xi)
-                        sum_im = sum_im + (qr * xi - qi * xr)
+                        for n in range(3):
+                            tap = taps[t, parity, n, a : a + 1, :]
+                            sums[n] = sums[n] + tap * shifted[n][a - k : a - k + 32]
                 lane = parity * 2 * TILE
-                work[s, pl.ds(at, 32), lane : lane + TILE] = sum_re
-                work[s, pl.ds(at, 32), lane + TILE : lane + 2 * TILE] = sum_im
+                work[s, pl.ds(at, 32), lane : lane + TILE] = sums[0] + sums[1]
+                work[s, pl.ds(at, 32), lane + TILE : lane + 2 * TILE] = sums[0] - sums[2]
             return inner
-
-        lax.fori_loop(0, rows // 32, fir, 0)
-
-        @pl.when(s == 0)
-        def _():
-            pair_copy(0).start()
 
         @pl.when(s == 1)
         def _():
             pair_copy(0).wait_recv()
-            for c in range(CHUNKS):
+
+        for c in range(CHUNKS):
+            lax.fori_loop(c * (chunk // 32), (c + 1) * (chunk // 32), fir, 0)
+
+            @pl.when(s == 1)
+            def _(c=c):
                 part = pl.ds(c * chunk, chunk)
                 work[1, part, :] = work[1, part, :] + pair_in[0, part, :]
                 read_copy(c).start()
 
-        @pl.when(s == 2)
+            @pl.when(s == 3)
+            def _(c=c):
+                if c == 0:
+                    pair_copy(1).wait_recv()
+                if c > 0:
+                    send(c - 1)
+
+        @pl.when(s % 2 == 0)
         def _():
-            pair_copy(1).start()
+            pair_copy(s // 2).start()
 
         return carry
 
-    lax.fori_loop(0, 4, step, 0)
-
-    pair_copy(1).wait_recv()
     lanes = lax.broadcasted_iota(jnp.int32, (32, TILE), 1) // share
-    for c in range(CHUNKS):
+
+    def send(c):
         read_copy(c).wait_recv()
 
-        def pack(i, carry, c=c):
+        def pack(i, carry):
             part = pl.ds(pl.multiple_of(c * chunk + i * 32, 32), 32)
             total = work[3, part, :] + pair_in[1, part, :] + read_in[part, :]
             quads = [total[:, q * TILE : (q + 1) * TILE] for q in (0, 2, 1, 3)]
@@ -387,6 +391,9 @@
         lax.fori_loop(0, chunk // 32, pack, 0)
         for d in range(1, freqs):
             freq_copy(d, c).start()
+
+    lax.fori_loop(0, 4, step, 0)
+    send(CHUNKS - 1)
     freq_in[f] = freq_out[f]
 
     wide = 2 * TILE
@@ -410,6 +417,8 @@
     for side in range(2):
         inverse[side] = total[:, side * TILE : (side + 1) * TILE]
 
+    for copy in col_copies:
+        copy.wait()
     for c in range(CHUNKS):
         for d in range(1, freqs):
             freq_copy(d, c).wait_recv()
@@ -427,19 +436,15 @@
                 sign = 1.0 if j == 1 else -1.0
                 top = even[:, :TILE] + sign * odd[:, TILE:]
                 low = even[:, TILE:] - sign * odd[:, :TILE]
-            for n, value in enumerate((top, low)):
-                hi, lo = split(value)
-                part = pl.ds(n * rows + c * chunk, chunk)
-                mixed[j, part, :TILE] = hi
-                mixed[j, part, TILE:] = lo
-    for copy in col_copies:
-        copy.wait()
-
-    for j in range(4):
-        both = dot(colh[j], mixed[j])
-        col_out[j] = both[:, :TILE] + both[:, TILE:] + dot(coll[j], mixed[j, :, :TILE])
-        for e in (1, 2, 0):
-            last_copy(e, j).start()
+            hi, lo = split(jnp.concatenate([top, low], axis=0))
+            at = c * 2 * chunk
+            both = dot(colh[j, :, at : at + 2 * chunk], jnp.concatenate([hi, lo], axis=1))
+            both = both[:, :TILE] + both[:, TILE:] + dot(coll[j, :, at : at + 2 * chunk], hi)
+            col_out[j] = both if c == 0 else col_out[j] + both
+            if c == CHUNKS - 1:
+                for e in (1, 2, 0):
+                    last_copy(e, j).start()
+
     lanes = lax.broadcasted_iota(jnp.int32, (TILE, TILE), 1)
     for j in range(4):
         last_in[reader, j] = col_out[j, pl.ds(pl.multiple_of(reader * TILE, TILE), TILE), :]
@@ -451,8 +456,12 @@
             im = jnp.where(lanes < TILE // 2, pltpu.roll(one, TILE // 2, 1), two)
             place = pl.ds(j, TILE, stride=4)
             gain = inverse[side, place, :]
-            out[0, side, place, :] = re * gain
-            out[1, side, place, :] = im * gain
+            stage[0, side, place, :] = re * gain
+            stage[1, side, place, :] = im * gain
+
+    for part in range(2):
+        for side in range(2):
+            out[part, :, side * TILE : (side + 1) * TILE] = stage[part, side]
 
     for n in range(2):
         pair_copy(n).wait_send()
@@ -484,9 +493,9 @@
     smem = pl.BlockSpec(memory_space=pltpu.SMEM)
     anywhere = pl.BlockSpec(memory_space=pl.ANY)
     dma = pltpu.SemaphoreType.DMA
-    result = pl.pallas_call(
+    return pl.pallas_call(
         functools.partial(fused_kernel, freqs),
-        out_shape=jax.ShapeDtypeStruct((2, 2, rows, TILE), F32),
+        out_shape=jax.ShapeDtypeStruct((2, rows, 2 * TILE), F32),
         in_specs=[smem] * 5 + [vmem] * 5 + [anywhere] * 5,
         out_specs=vmem,
         scratch_shapes=[
@@ -501,10 +510,10 @@
             pltpu.VMEM((rows, 4 * TILE), F32),
             pltpu.VMEM((freqs, rows, TILE), F32),
             pltpu.VMEM((freqs, rows, TILE), F32),
-            pltpu.VMEM((4, 2, 2, stamp_len, TILE), F32),
+            pltpu.VMEM((4, 2, 3, stamp_len, TILE), F32),
             pltpu.VMEM((4, rows, 2 * rows), BF16),
             pltpu.VMEM((4, rows, 2 * rows), BF16),
-            pltpu.VMEM((4, 2 * rows, 2 * TILE), BF16),
+            pltpu.VMEM((2, 2, rows, TILE), F32),
             pltpu.VMEM((4, rows, TILE), F32),
             pltpu.VMEM((4, 4, TILE, TILE), F32),
             pltpu.VMEM((2, rows, TILE), F32),
@@ -528,18 +537,19 @@
         name="fused",
     )(
         *scalars, stamps, tap_table, psf_rows, psf_cols, order, block,
-        *row_tables(ids, width), *column_tables(height),
+        *row_tables(ids, width), *column_tables(height, CHUNKS),
     )
-    return result.transpose(0, 2, 1, 3).reshape(2, rows, 2 * TILE)
-
-
-def column_tables(height):
+
+
+def column_tables(height, chunks=1):
     quarter = height // 4
     inner = np.arange(quarter)
     parts = []
     for j in range(4):
         phase = angles(4 * np.arange(quarter) + j, inner, height)
-        parts.append(np.concatenate([np.cos(phase), np.sin(phase)], axis=1))
+        both = np.stack([np.cos(phase), np.sin(phase)], axis=1)
+        both = both.reshape(quarter, 2, chunks, -1).transpose(0, 2, 1, 3)
+        parts.append(both.reshape(quarter, -1))
     return split_np(np.stack(parts))
 
 

time: 81.3 us -> 81 us (level)
    unnamed x1 -> x2, local copies, waits for them, and re-layouts: 1.34 us -> 3.6 us
    transpose x1 -> x0, local copies, waits for them, and re-layouts: 1.56 us -> none  [fused(): return result.transpose(0, 2, 1, 3).reshape(2, rows, 2 * TILE)]
    reshape x1 -> x0, local copies, waits for them, and re-layouts: 1.31 us -> none  [fused(): return result.transpose(0, 2, 1, 3).reshape(2, rows, 2 * TILE)]
where the time goes in v4:
time: 81 us; the launch traced here: 80.8 us
  Pallas kernels  77.2 us (95%)
  local copies, waits for them, and re-layouts  3.6 us (4%)
    pallas_call x1, Pallas kernels, fused(): pl.pallas_call(functools.partial(fused_kernel, freqs), out_shape=jax.Shap...  77.2 us
    unnamed x2, local copies, waits for them, and re-layouts  3.6 us

profile of v4, /device:TPU:0, one launch (start us, length us, event | category | flops | bytes accessed | tf_op | source)
XLA Modules:
  0.0 80.8 jit_solution(6881906487203152255)
XLA Ops:
  0.0 1.3 %copy.16.footprint = s32[4,2]{1,0:T(4,128)} copy(s32[4,2]{0,1:T(2,128)} %param.19) | data formatting | bytes 64 | tf_op args[4]
  1.3 77.2 %fused.1 = f32[2,512,256]{2,1,0:T(8,128)} custom-call(s32[4]{0:T(128)} %assign.1, s32[4,2]{1,0:T(4,128)} %copy.16.footprint, s32[4]{0:T(128)} %accept.1, f32[4]{0:T(128)} %zero_point.1, f32[4]{0:T(128)} %noise_var.1, f32[4,16,16]{2,1,0:T(8,128)} %stamps.1, f32[16,2048]{1,0:T(8,128)} %constant.16.clone.tap_table, f32[4,512,32]{2,1,0:T(8,128)} %constant.17.clone.psf_rows, ...), custom_call_target="tpu_custom_call" | custom-call | tf_op jit(solution)/shard_map/fused/pallas_call | solution.py:496
  78.5 2.3 %copy.18 = f32[2,512,256]{2,1,0:T(8,128)} copy(f32[2,512,256]{2,1,0:T(8,128)} %fused.1) | data formatting | bytes 2097152

commit v5 on v4

--- a/solution.py
+++ b/solution.py
@@ -159,7 +159,7 @@
     )(info, low, block, high, taps, *tables)
 
 
-CHUNKS = 4
+CHUNKS = 8
 MESH = pl.DeviceIdType.MESH
 
 

time: 81 us -> 79.8 us (0.985)
  Pallas kernels: 77.2 us -> 76 us
    pallas_call x1, Pallas kernels: 77.2 us -> 76 us  [fused(): pl.pallas_call(functools.partial(fused_kernel, freqs), out_shape=jax.Shap...]
where the time goes in v5:
time: 79.8 us; the launch traced here: 79.6 us
  Pallas kernels  76 us (95%)
  local copies, waits for them, and re-layouts  3.6 us (5%)
    pallas_call x1, Pallas kernels, fused(): pl.pallas_call(functools.partial(fused_kernel, freqs), out_shape=jax.Shap...  76 us
    unnamed x2, local copies, waits for them, and re-layouts  3.6 us

profile of v5, /device:TPU:0, one launch (start us, length us, event | category | flops | bytes accessed | tf_op | source)
XLA Modules:
  0.0 79.6 jit_solution(14645924616545918013)
XLA Ops:
  0.0 1.3 %copy.16.footprint = s32[4,2]{1,0:T(4,128)} copy(s32[4,2]{0,1:T(2,128)} %param.19) | data formatting | bytes 64 | tf_op args[4]
  1.3 76.0 %fused.1 = f32[2,512,256]{2,1,0:T(8,128)} custom-call(s32[4]{0:T(128)} %assign.1, s32[4,2]{1,0:T(4,128)} %copy.16.footprint, s32[4]{0:T(128)} %accept.1, f32[4]{0:T(128)} %zero_point.1, f32[4]{0:T(128)} %noise_var.1, f32[4,16,16]{2,1,0:T(8,128)} %stamps.1, f32[16,2048]{1,0:T(8,128)} %constant.16.clone.tap_table, f32[4,512,32]{2,1,0:T(8,128)} %constant.17.clone.psf_rows, ...), custom_call_target="tpu_custom_call" | custom-call | tf_op jit(solution)/shard_map/fused/pallas_call | solution.py:496
  77.3 2.3 %copy.18 = f32[2,512,256]{2,1,0:T(8,128)} copy(f32[2,512,256]{2,1,0:T(8,128)} %fused.1) | data formatting | bytes 2097152
